TPU v7x, 32 devices: a whole 2x2x4 slice. The times are simulated.
32 devices in a mesh: blk: 16 (over z, y, core), cset: 2 (over x).
Axes of the slice: x: 2, y: 2, z: 4, core: 2. Of those that a mesh axis runs over, the one named last changes fastest.
Arguments:
- active_table: bfloat16 [8192, 256], P(('blk', 'cset')), may hold values from 0.019897461 to 0.19921875
- passive_table: bfloat16 [8192, 256], P(('blk', 'cset')), may hold values from 0 to 0.15
- adjacency: bfloat16 [16, 2, 5, 8, 128, 128], P('blk', 'cset'), may hold values from 0 to 1, as said below
- tile_dst: int32 [16, 2, 5, 8], P('blk', 'cset'), may hold values from 0 to 1
- tile_src: int32 [16, 2, 5, 8], P('blk', 'cset'), may hold values from 0 to 3
- tile_count: int32 [16, 2, 5], P('blk', 'cset'), may hold values from 1 to 8, as said below
- split_active: int32 [20, 924], replicated, may hold values from 0 to 219, as said below
- split_passive: int32 [20, 924], replicated, may hold values from 0 to 219, as said below
Outputs:
- joined_table: bfloat16 [8192, 1024], P('blk', 'cset')
Inputs may be any that keep to these rules, and one draw needn't show every extreme that they name: For each six-color set s, the 20 pairs (split_active[j, s], split_passive[j, s]) name its 20 divisions into an ordered pair of three-color sets, each once, as columns of the two child tables; a child table's columns hold its 220 color sets in some fixed order, and columns 220 and above are never named. `split_passive`: see split_active; each table is a column order of its own. `tile_count`: the own partition's slot r = 2 is full on every device. `adjacency`: edge weights are 0 or 1.
All inputs are finite; a program needn't handle non-finite values.
Results may differ from a plain program's by a relative error of at most 0.0026.
Values may be sent and summed in bfloat16 or wider, within the bound.
A program may use at most 64 MiB of HBM per device.

v0:
```python
import jax
import jax.numpy as jnp
from jax import lax
from jax.sharding import PartitionSpec as P

SPLITS = 20
OUTPAD = 1024
TILE = 128


def shifted(block, axis, distance):
    devices = range(lax.axis_size(axis))
    route = [((i - distance) % len(devices), i) for i in devices]
    return lax.ppermute(block, axis, route)


def add_partition(accumulated, incoming, slot, tiles_all, dst_all, src_all, count_all):
    tiles = lax.dynamic_index_in_dim(tiles_all, slot, 0, keepdims=False)
    dst_rows = lax.dynamic_index_in_dim(dst_all, slot, 0, keepdims=False)
    src_rows = lax.dynamic_index_in_dim(src_all, slot, 0, keepdims=False)
    count_now = lax.dynamic_index_in_dim(count_all, slot, 0, keepdims=False)
    blocks = incoming.reshape(incoming.shape[0] // TILE, TILE, incoming.shape[1])
    chosen = jnp.take(blocks, src_rows, axis=0)
    live = (jnp.arange(tiles.shape[0], dtype=jnp.int32) < count_now).astype(jnp.bfloat16)
    masked = tiles * live[:, None, None]
    product = jnp.einsum("tij,tjc->tic", masked, chosen, preferred_element_type=jnp.float32)
    row_tiles = accumulated.shape[0] // TILE
    placing = (dst_rows[:, None] == jnp.arange(row_tiles, dtype=jnp.int32)[None, :]).astype(
        jnp.float32
    )
    summed = jnp.einsum("td,tic->dic", placing, product, precision=lax.Precision.HIGHEST)
    return accumulated + summed.reshape(accumulated.shape)


def combine_sets(left, right, left_cols, right_cols):
    channel = jnp.arange(left.shape[1], dtype=jnp.int32)
    joined = jnp.zeros((left.shape[0], left_cols.shape[1]), jnp.float32)
    for split in range(SPLITS):
        pick_left = (left_cols[split][None, :] == channel[:, None]).astype(jnp.bfloat16)
        pick_right = (right_cols[split][None, :] == channel[:, None]).astype(jnp.bfloat16)
        joined = joined + jnp.dot(left, pick_left, preferred_element_type=jnp.float32) * jnp.dot(
            right, pick_right, preferred_element_type=jnp.float32
        )
    return joined.astype(jnp.bfloat16)


def local(
    active_table,
    passive_table,
    adjacency,
    tile_dst,
    tile_src,
    tile_count,
    split_active,
    split_passive,
):
    tiles_all = adjacency[0, 0]
    dst_all = tile_dst[0, 0]
    src_all = tile_src[0, 0]
    count_all = tile_count[0, 0]
    reach_half = (tiles_all.shape[0] - 1) // 2
    partition_rows = lax.all_gather(passive_table, "cset", axis=0, tiled=True)
    accumulated = jnp.zeros((passive_table.shape[0], passive_table.shape[1]), jnp.float32)
    accumulated = add_partition(
        accumulated, partition_rows, reach_half, tiles_all, dst_all, src_all, count_all
    )

    def upward(step, state):
        moving, summed = state
        moving = shifted(moving, "blk", 1)
        summed = add_partition(
            summed, moving, reach_half - step, tiles_all, dst_all, src_all, count_all
        )
        return (moving, summed)

    def downward(step, state):
        moving, summed = state
        moving = shifted(moving, "blk", -1)
        summed = add_partition(
            summed, moving, reach_half + step, tiles_all, dst_all, src_all, count_all
        )
        return (moving, summed)

    moved, accumulated = lax.fori_loop(1, reach_half + 1, upward, (partition_rows, accumulated))
    moved, accumulated = lax.fori_loop(1, reach_half + 1, downward, (partition_rows, accumulated))
    neighbour = accumulated.astype(jnp.bfloat16)
    extra = OUTPAD - split_active.shape[1]
    left_cols = jnp.pad(split_active, ((0, 0), (0, extra)), constant_values=-1)
    right_cols = jnp.pad(split_passive, ((0, 0), (0, extra)), constant_values=-1)
    wide_active, wide_neighbour = (
        lax.all_gather(active_table, "cset", axis=0, tiled=True),
        lax.all_gather(neighbour, "cset", axis=0, tiled=True),
    )
    width = OUTPAD // lax.axis_size("cset")
    start = lax.axis_index("cset") * width
    own_left = lax.dynamic_slice_in_dim(left_cols, start, width, 1)
    own_right = lax.dynamic_slice_in_dim(right_cols, start, width, 1)
    return combine_sets(wide_active, wide_neighbour, own_left, own_right)


def solution(mesh):
    in_specs = (
        P(("blk", "cset"), None),
        P(("blk", "cset"), None),
        P("blk", "cset", None, None, None, None),
        P("blk", "cset", None, None),
        P("blk", "cset", None, None),
        P("blk", "cset", None),
        P(),
        P(),
    )
    out_specs = P("blk", "cset")
    return jax.shard_map(local, mesh=mesh, in_specs=in_specs, out_specs=out_specs, check_vma=False)
```

profile of v0, /device:TPU:0, one launch (start us, length us, event | category | flops | bytes accessed | tf_op | source)
XLA Modules:
  0.0 79.6 jit_solution(13007456574544450492)
XLA Ops:
  0.0 7.5 %all_gather.10 = bf16[512,256]{1,0:T(8,128)(2,1)S(1)} all-gather(bf16[256,256]{1,0:T(8,128)(2,1)} %param.15), channel_id=1, replica_groups=mesh['blk'=16,'cset'=2] {'cset'}, dimensions={0}, use_global_device_ids=true | all-gather | bytes 393216 | tf_op jit(solution)/shard_map/all_gather | solution.py:62
  7.5 1.2 %dynamic_slice.131 = s32[1,1,1]{2,1,0:T(1,128)} slice(s32[1,1,5]{2,1,0:T(1,128)} %param.19), slice={[0:1], [0:1], [2:3]} | slice | bytes 8 | tf_op jit(solution)/shard_map/jit(dynamic_index_in_dim)/dynamic_slice | solution.py:21
  8.7 1.3 %compare_and_fusion.2 = (pred[8]{0:T(512)(128)(4,1)S(1)}, s32[8]{0:T(128)S(1)}, bf16[8]{0:T(256)(128)(2,1)S(1)}) fusion(s32[1,1,5,8]{3,1,2,0:T(1,128)} %param.18, s32[]{:T(128)} %bitcast.19), kind=kLoop, calls=%fused_computation.245 | loop fusion | flops 64 | bytes 92 | tf_op jit(solution)/shard_map/jit(_take)/and | solution.py:23
  10.0 0.6 gather_fusion.2
  11.1 1.2 %fusion.72 = f32[2,128,256]{2,0,1:T(2,128)S(1)} fusion(f32[8,128,256]{2,1,0:T(8,128)S(1)} %fusion.74, s32[8]{0:T(128)S(1)} %slice_bitcast_fusion), kind=kOutput, calls=%fused_computation.111 | convolution fusion | flops 6291472 | bytes 1310752 | tf_op jit(solution)/shard_map/td,tic->dic/dot_general | solution.py:31
  12.3 21.6 %while.38 = (s32[]{:T(128)}, bf16[512,256]{1,0:T(8,128)(2,1)S(1)}, f32[256,256]{1,0:T(8,128)S(1)}, s32[5,8]{1,0:T(8,128)S(1)}, bf16[5,8,128,128]{3,2,1,0:T(8,128...) while((s32[]{:T(128)}, bf16[512,256]{1,0:T(8,128)(2,1)S(1)}, ...), condition=%wide.region_1.3_spmd, body=%wide.region_0.2_spmd.sunk | while | flops 73860184 | bytes 7083479 | solution.py:84
  12.4 0.6 dynamic_slice.175
  13.0 0.6 compare_and_fusion.5
  13.7 7.2 %collective-permute-done = bf16[512,256]{1,0:T(8,128)(2,1)S(1)} collective-permute-done((bf16[512,256]{1,0:T(8,128)(2,1)S(1)}, bf16[512,256]{1,0:T(8,128)(2,1)S(1)}, u32[]{:S(2)}, u32[]{:S(2)}) %collective-permute-start) | collective-permute-done | bytes 262176 | tf_op jit(solution)/shard_map/while/body/eval_jaxpr/ppermute | solution.py:14
  20.9 0.6 gather_fusion
  21.5 0.4 fusion.240
  21.8 1.2 %fusion.242 = f32[2,128,256]{2,0,1:T(2,128)S(1)} fusion(f32[8,128,256]{2,1,0:T(8,128)S(1)} %fusion.240, s32[8]{0:T(128)S(1)} %fusion.241), kind=kOutput, calls=%fused_computation.3.clone.1 | convolution fusion | flops 6291472 | bytes 1310752 | tf_op jit(solution)/shard_map/while/body/eval_jaxpr/td,tic->dic/dot_general | solution.py:31
  23.2 0.6 dynamic_slice.175
  23.8 0.6 compare_and_fusion.5
  24.5 7.2 %collective-permute-done = bf16[512,256]{1,0:T(8,128)(2,1)S(1)} collective-permute-done((bf16[512,256]{1,0:T(8,128)(2,1)S(1)}, bf16[512,256]{1,0:T(8,128)(2,1)S(1)}, u32[]{:S(2)}, u32[]{:S(2)}) %collective-permute-start) | collective-permute-done | bytes 262176 | tf_op jit(solution)/shard_map/while/body/eval_jaxpr/ppermute | solution.py:14
  31.7 0.6 gather_fusion
  32.7 1.2 %fusion.242 = f32[2,128,256]{2,0,1:T(2,128)S(1)} fusion(f32[8,128,256]{2,1,0:T(8,128)S(1)} %fusion.240, s32[8]{0:T(128)S(1)} %fusion.241), kind=kOutput, calls=%fused_computation.3.clone.1 | convolution fusion | flops 6291472 | bytes 1310752 | tf_op jit(solution)/shard_map/while/body/eval_jaxpr/td,tic->dic/dot_general | solution.py:31
  34.0 17.0 %while.39 = (s32[]{:T(128)}, bf16[512,256]{1,0:T(8,128)(2,1)S(1)}, f32[256,256]{1,0:T(8,128)S(1)}, s32[5,8]{1,0:T(8,128)S(1)}, bf16[5,8,128,128]{3,2,1,0:T(8,128...) while((s32[]{:T(128)}, bf16[512,256]{1,0:T(8,128)(2,1)S(1)}, ...), condition=%wide.region_3.5_spmd, body=%wide.region_2.4_spmd.sunk | while | flops 73860184 | bytes 7083479 | solution.py:85
  34.1 0.6 dynamic_slice.178
  34.7 0.6 compare_and_fusion.6
  35.3 2.6 %collective-permute-done.1 = bf16[512,256]{1,0:T(8,128)(2,1)S(1)} collective-permute-done((bf16[512,256]{1,0:T(8,128)(2,1)S(1)}, bf16[512,256]{1,0:T(8,128)(2,1)S(1)}, u32[]{:S(2)}, u32[]{:S(2)}) %collective-permute-start.1) | collective-permute-done | bytes 262176 | tf_op jit(solution)/shard_map/while/body/eval_jaxpr/ppermute | solution.py:14
  37.9 0.6 gather_fusion.1
  38.9 1.2 %fusion.248 = f32[2,128,256]{2,0,1:T(2,128)S(1)} fusion(f32[8,128,256]{2,1,0:T(8,128)S(1)} %fusion.246, s32[8]{0:T(128)S(1)} %fusion.247), kind=kOutput, calls=%fused_computation.27.clone.1 | convolution fusion | flops 6291472 | bytes 1310752 | tf_op jit(solution)/shard_map/while/body/eval_jaxpr/td,tic->dic/dot_general | solution.py:31
  40.2 4.7 %collective-permute-start.1 = (bf16[512,256]{1,0:T(8,128)(2,1)S(1)}, bf16[512,256]{1,0:T(8,128)(2,1)S(1)}, u32[]{:S(2)}, u32[]{:S(2)}) collective-permute-start(bf16[512,256]{1,0:T(8,128)(2,1)S(1)} %get-tuple-element.688), channel_id=1, source_target_pairs={{2,0},{4,2},{6,4},{8,6},{10,8},{12,10},{14,12},{16,14},{18,16},{20... | collective-permute-start | bytes 786440 | tf_op jit(solution)/shard_map/while/body/eval_jaxpr/ppermute | solution.py:14
  44.9 0.6 dynamic_slice.178
  45.5 0.6 compare_and_fusion.6
  46.1 2.6 %collective-permute-done.1 = bf16[512,256]{1,0:T(8,128)(2,1)S(1)} collective-permute-done((bf16[512,256]{1,0:T(8,128)(2,1)S(1)}, bf16[512,256]{1,0:T(8,128)(2,1)S(1)}, u32[]{:S(2)}, u32[]{:S(2)}) %collective-permute-start.1) | collective-permute-done | bytes 262176 | tf_op jit(solution)/shard_map/while/body/eval_jaxpr/ppermute | solution.py:14
  48.8 0.6 gather_fusion.1
  49.7 1.2 %fusion.248 = f32[2,128,256]{2,0,1:T(2,128)S(1)} fusion(f32[8,128,256]{2,1,0:T(8,128)S(1)} %fusion.246, s32[8]{0:T(128)S(1)} %fusion.247), kind=kOutput, calls=%fused_computation.27.clone.1 | convolution fusion | flops 6291472 | bytes 1310752 | tf_op jit(solution)/shard_map/while/body/eval_jaxpr/td,tic->dic/dot_general | solution.py:31
  51.0 6.5 %all_gather.11 = bf16[512,256]{1,0:T(8,128)(2,1)S(1)} all-gather(bf16[256,256]{1,0:T(8,128)(2,1)S(1)} %convert_element_type.51), channel_id=1, replica_groups=mesh['blk'=16,'cset'=2] {'cset'}, dimensions={0}, use_global_device_ids=true | all-gather | bytes 393216 | tf_op jit(solution)/shard_map/all_gather | solution.py:92
  58.0 5.8 %all_gather.9 = bf16[512,256]{1,0:T(8,128)(2,1)S(1)} all-gather(bf16[256,256]{1,0:T(8,128)(2,1)S(1)} %copy-done.3), channel_id=1, replica_groups=mesh['blk'=16,'cset'=2] {'cset'}, dimensions={0}, use_global_device_ids=true | all-gather | bytes 393216 | tf_op jit(solution)/shard_map/all_gather | solution.py:91
  78.6 1.0 %copy.53 = bf16[512,512]{1,0:T(8,128)(2,1)} copy(bf16[512,512]{0,1:T(8,128)(2,1)S(1)} %fusion.71) | data formatting | bytes 1048576 | tf_op jit(solution)/shard_map/convert_element_type | solution.py:44
  (94 shorter events, 17.0 us)
Async XLA Ops:
  0.0 10.6 %copy-start = (bf16[1,1,5,8,128,128]{5,4,3,2,1,0:T(8,128)(2,1)S(1)}, bf16[1,1,5,8,128,128]{5,4,3,2,1,0:T(8,128)(2,1)}, u32[]{:S(2)}) copy-start(bf16[1,1,5,8,128,128]{5,4,3,2,1,0:T(8,128)(2,1)} %param.16) | copy-start | bytes 3932164
  10.0 1.0 %copy-start.5 = (s32[1,1,5,8]{3,1,2,0:T(1,128)S(1)}, s32[1,1,5,8]{3,1,2,0:T(1,128)}, u32[]{:S(2)}) copy-start(s32[1,1,5,8]{3,1,2,0:T(1,128)} %param.17) | copy-start | bytes 484
  11.0 1.3 %copy-start.4 = (s32[1,1,5,8]{3,1,2,0:T(1,128)S(1)}, s32[1,1,5,8]{3,1,2,0:T(1,128)}, u32[]{:S(2)}) copy-start(s32[1,1,5,8]{3,1,2,0:T(1,128)} %param.18) | copy-start | bytes 484
  11.0 1.3 %copy-start.6 = (s32[1,1,5]{2,1,0:T(1,128)S(1)}, s32[1,1,5]{2,1,0:T(1,128)}, u32[]{:S(2)}) copy-start(s32[1,1,5]{2,1,0:T(1,128)} %param.19) | copy-start | bytes 64
  12.3 8.5 %collective-permute-start = (bf16[512,256]{1,0:T(8,128)(2,1)S(1)}, bf16[512,256]{1,0:T(8,128)(2,1)S(1)}, u32[]{:S(2)}, u32[]{:S(2)}) collective-permute-start(bf16[512,256]{1,0:T(8,128)(2,1)S(1)} %get-tuple-element.655), channel_id=1, source_target_pairs={{30,0},{0,2},{2,4},{4,6},{6,8},{8,10},{10,12},{12,14},{14,16},{16,... | collective-permute-start | bytes 786440 | tf_op jit(solution)/shard_map/while/body/eval_jaxpr/ppermute | solution.py:14
  23.1 8.5 %collective-permute-start = (bf16[512,256]{1,0:T(8,128)(2,1)S(1)}, bf16[512,256]{1,0:T(8,128)(2,1)S(1)}, u32[]{:S(2)}, u32[]{:S(2)}) collective-permute-start(bf16[512,256]{1,0:T(8,128)(2,1)S(1)} %get-tuple-element.655), channel_id=1, source_target_pairs={{30,0},{0,2},{2,4},{4,6},{6,8},{8,10},{10,12},{12,14},{14,16},{16,... | collective-permute-start | bytes 786440 | tf_op jit(solution)/shard_map/while/body/eval_jaxpr/ppermute | solution.py:14
  34.0 23.6 %copy-start.1 = (s32[20,924]{1,0:T(8,128)S(1)}, s32[20,924]{1,0:T(8,128)}, u32[]{:S(2)}) copy-start(s32[20,924]{1,0:T(8,128)} %param.21) | copy-start | bytes 221764
  34.0 23.6 %copy-start.2 = (s32[20,924]{1,0:T(8,128)S(1)}, s32[20,924]{1,0:T(8,128)}, u32[]{:S(2)}) copy-start(s32[20,924]{1,0:T(8,128)} %param.20) | copy-start | bytes 221764
  34.0 3.9 %collective-permute-start.1 = (bf16[512,256]{1,0:T(8,128)(2,1)S(1)}, bf16[512,256]{1,0:T(8,128)(2,1)S(1)}, u32[]{:S(2)}, u32[]{:S(2)}) collective-permute-start(bf16[512,256]{1,0:T(8,128)(2,1)S(1)} %get-tuple-element.688), channel_id=1, source_target_pairs={{2,0},{4,2},{6,4},{8,6},{10,8},{12,10},{14,12},{16,14},{18,16},{20... | collective-permute-start | bytes 786440 | tf_op jit(solution)/shard_map/while/body/eval_jaxpr/ppermute | solution.py:14
  40.2 8.5 %collective-permute-start.1 = (bf16[512,256]{1,0:T(8,128)(2,1)S(1)}, bf16[512,256]{1,0:T(8,128)(2,1)S(1)}, u32[]{:S(2)}, u32[]{:S(2)}) collective-permute-start(bf16[512,256]{1,0:T(8,128)(2,1)S(1)} %get-tuple-element.688), channel_id=1, source_target_pairs={{2,0},{4,2},{6,4},{8,6},{10,8},{12,10},{14,12},{16,14},{18,16},{20... | collective-permute-start | bytes 786440 | tf_op jit(solution)/shard_map/while/body/eval_jaxpr/ppermute | solution.py:14
  51.0 7.0 %copy-start.3 = (bf16[256,256]{1,0:T(8,128)(2,1)S(1)}, bf16[256,256]{1,0:T(8,128)(2,1)}, u32[]{:S(2)}) copy-start(bf16[256,256]{1,0:T(8,128)(2,1)} %param.14) | copy-start | bytes 393220
where the time goes:
time: 79.8 us; the launch traced here: 79.6 us
  matrix products  21.8 us (27%)
  blocking collectives  19.8 us (25%)
  waiting for transfers between devices  19.6 us (25%)
  local copies, waits for them, and re-layouts  8.59 us (11%)
  starting transfers between devices  4.83 us (6%)
  other arithmetic  4.1 us (5%)
    ppermute x4, waiting for transfers between devices, shifted(): return lax.ppermute(block, axis, route)  19.6 us
    all_gather x1, blocking collectives, local(): partition_rows = lax.all_gather(passive_table, 'cset', axis=0, tiled=True)  7.48 us
    dot_general x20, matrix products, combine_sets(): jnp.dot(right, pick_right, preferred_element_type=jnp.float32)  7.06 us
    dot_general x20, matrix products, combine_sets(): jnp.dot(left, pick_left, preferred_element_type=jnp.float32)  7.03 us
    all_gather x1, blocking collectives, local(): lax.all_gather(neighbour, 'cset', axis=0, tiled=True)  6.53 us
    dot_general x5, matrix products, add_partition(): jnp.einsum('td,tic->dic', placing, product, precision=lax.Precision.HIGHEST)  5.83 us
    all_gather x1, blocking collectives, local(): lax.all_gather(active_table, 'cset', axis=0, tiled=True)  5.83 us
    ppermute x4, starting transfers between devices, shifted(): return lax.ppermute(block, axis, route)  4.83 us
  transfers between devices with their start and end apart: 4, of which 4 were waited for; matrix products, arithmetic and copies ran while one was open for 6% of the time, Pallas kernels for 0%

commit v1 on v0

v1 whole, which is shorter than its diff:
```python
import functools

import jax
import jax.numpy as jnp
from jax import lax
from jax.experimental import pallas as pl
from jax.experimental.pallas import tpu as pltpu
from jax.sharding import PartitionSpec as P

OUTPAD = 1024
TILE = 128
MESH = pl.DeviceIdType.MESH


def kernel(
    n_blk,
    n_cset,
    half,
    dst_s,
    src_s,
    count_s,
    active_h,
    passive_h,
    adjacency_h,
    left_h,
    right_h,
    out_h,
    active_v,
    left_raw,
    right_raw,
    left_v,
    right_v,
    tiles_v,
    dense_v,
    picked_v,
    choose_v,
    neighbour_v,
    result_v,
    *rest,
):
    home = rest[: half + 1]
    away = (None,) + rest[half + 1 : 2 * half + 1]
    (
        local_sem,
        own_send,
        side_send,
        sibling_send,
        home_recv,
        away_recv,
        out_send,
        out_recv,
        out_local,
    ) = rest[2 * half + 1 :]
    b = lax.axis_index("blk")
    c = lax.axis_index("cset")
    rows, channels = active_v.shape
    splits, sets = left_raw.shape
    width = out_h.shape[1]
    piece = min(width, 256)
    sign = 2 * (b % 2) - 1
    sibling = (b - sign, c)
    others = [(c + i) % n_cset for i in range(1, n_cset)]
    targets = [None] + [
        ((b + k * (1 - 2 * ((b - k + n_blk) % 2)) + n_blk) % n_blk, c) for k in range(1, half + 1)
    ]
    sources = [None] + [((b + sign * k + n_blk) % n_blk, c) for k in range(1, half + 1)]

    barrier = pltpu.get_barrier_semaphore()
    senders = sources[1:] + [sibling] + [(b, o) for o in others]
    for device in senders:
        pl.semaphore_signal(barrier, inc=1, device_id=device, device_id_type=MESH)

    mine = pl.ds(pl.multiple_of(c * rows, rows), rows)
    copies = [
        pltpu.make_async_copy(left_h, left_raw, local_sem.at[0]),
        pltpu.make_async_copy(right_h, right_raw, local_sem.at[1]),
        pltpu.make_async_copy(active_h, active_v, local_sem.at[2]),
        pltpu.make_async_copy(adjacency_h, tiles_v, local_sem.at[3]),
        pltpu.make_async_copy(passive_h, home[0].at[mine, :], local_sem.at[4]),
    ]
    for copy in copies:
        copy.start()
    pl.semaphore_wait(barrier, len(senders))

    started = []

    def part(cset):
        return pl.ds(pl.multiple_of(cset * rows, rows), rows)

    def send(src, dst, send_sem, recv_sem, device):
        copy = pltpu.make_async_remote_copy(
            src_ref=src,
            dst_ref=dst,
            send_sem=send_sem,
            recv_sem=recv_sem,
            device_id=device,
            device_id_type=MESH,
        )
        copy.start()
        started.append(copy)

    def to_others(block, k):
        for i, other in enumerate(others):
            send(block, home[k].at[mine, :], side_send.at[k, i], home_recv.at[k, c], (b, other))

    def to_sibling(block, k, cset):
        send(
            block,
            away[k + 1].at[part(cset), :],
            sibling_send.at[k, cset],
            away_recv.at[k, cset],
            sibling,
        )

    def arrived(ref, cset, sem):
        pltpu.make_async_copy(ref.at[part(cset), :], ref.at[part(cset), :], sem).wait()

    for k in range(half, 0, -1):
        send(passive_h, home[k].at[mine, :], own_send.at[k], home_recv.at[k, c], targets[k])
    to_others(passive_h, 0)
    to_sibling(passive_h, 0, c)

    copies[0].wait()
    copies[1].wait()
    left_v[...] = jnp.full(left_v.shape, -1, jnp.int32)
    right_v[...] = jnp.full(right_v.shape, -1, jnp.int32)
    left_v[:splits, :sets] = left_raw[...]
    right_v[:splits, :sets] = right_raw[...]
    copies[2].wait()
    copies[3].wait()

    def assemble(r, carry):
        for d in range(rows // TILE):
            for e in range(n_cset * rows // TILE):
                total = jnp.zeros((TILE, TILE), jnp.bfloat16)
                for t in range(tiles_v.shape[1]):
                    here = (dst_s[r, t] == d) & (src_s[r, t] == e) & (count_s[r] > t)
                    total = total + jnp.where(here, tiles_v[r, t], jnp.zeros_like(total))
                dense_v[r, d * TILE : (d + 1) * TILE, e * TILE : (e + 1) * TILE] = total
        return carry

    channel = lax.broadcasted_iota(jnp.int32, (channels, 256), 0)

    def pick(j, carry):
        for at in range(0, OUTPAD, 256):
            columns = slice(at, at + 256)
            left_one = (left_v[pl.ds(j, 1), columns] == channel).astype(jnp.bfloat16)
            right_one = (right_v[pl.ds(j, 1), columns] == channel).astype(jnp.bfloat16)
            choose_v[j, :, columns] = right_one
            picked = jnp.dot(active_v[...], left_one, preferred_element_type=jnp.float32)
            picked_v[j, :, columns] = picked.astype(jnp.bfloat16)
        return carry

    def side_arrived(k):
        for other in others:
            arrived(home[k], other, home_recv.at[k, other])
            if k < half:
                to_sibling(home[k].at[part(other), :], k, other)

    def own_arrived(k):
        arrived(home[k], c, home_recv.at[k, c])
        to_others(home[k].at[mine, :], k)
        if k < half:
            to_sibling(home[k].at[mine, :], k, c)

    stages = [functools.partial(own_arrived, 1), functools.partial(side_arrived, 0)]
    for k in range(2, half + 1):
        stages += [functools.partial(own_arrived, k), functools.partial(side_arrived, k - 1)]

    lax.fori_loop(0, 2 * half + 1, assemble, 0)
    for i, stage in enumerate(stages):
        lax.fori_loop(splits * i // len(stages), splits * (i + 1) // len(stages), pick, 0)
        stage()

    def times(r, ref):
        return jnp.dot(dense_v[r], ref[...], preferred_element_type=jnp.float32)

    copies[4].wait()
    total = times(half, home[0])
    for k in range(1, half):
        total = total + times(half + sign * k, home[k])
    for k in range(1, half + 1):
        for cset in [c] + others:
            arrived(away[k], cset, away_recv.at[k - 1, cset])
        total = total + times(half - sign * k, away[k])
    side_arrived(half)
    total = total + times(half + sign * half, home[half])
    neighbour_v[...] = total.astype(jnp.bfloat16)

    results = []
    for i, owner in enumerate(others + [c]):
        for p in range(width // piece):
            columns = pl.ds(pl.multiple_of(owner * width + p * piece, piece), piece)

            def step(g, total):
                for u in range(4):
                    j = g * 4 + u
                    found = jnp.dot(
                        neighbour_v[...],
                        choose_v[j, :, columns],
                        preferred_element_type=jnp.float32,
                    )
                    total = total + picked_v[j, :, columns].astype(jnp.float32) * found
                return total

            total = lax.fori_loop(0, splits // 4, step, jnp.zeros((rows, piece), jnp.float32))
            result_v[i, :, p * piece : (p + 1) * piece] = total.astype(jnp.bfloat16)
            block = result_v.at[i, :, pl.ds(p * piece, piece)]
            goal = out_h.at[mine, pl.ds(p * piece, piece)]
            if i < n_cset - 1:
                send(block, goal, out_send.at[i, p], out_recv.at[c, p], (b, owner))
            else:
                copy = pltpu.make_async_copy(block, goal, out_local.at[p])
                copy.start()
                results.append(copy)
    for copy in results:
        copy.wait()
    for copy in started:
        copy.wait_send()
    for other in others:
        for p in range(width // piece):
            block = out_h.at[part(other), pl.ds(p * piece, piece)]
            pltpu.make_async_copy(block, block, out_recv.at[other, p]).wait()


def local(
    active_table,
    passive_table,
    adjacency,
    tile_dst,
    tile_src,
    tile_count,
    split_active,
    split_passive,
):
    n_blk, n_cset = lax.axis_size("blk"), lax.axis_size("cset")
    rows, channels = passive_table.shape
    tiles = adjacency[0, 0]
    reach, slots = tiles.shape[:2]
    half = (reach - 1) // 2
    splits, sets = split_active.shape
    width = OUTPAD // n_cset
    pieces = width // min(width, 256)
    hbm = pl.BlockSpec(memory_space=pl.ANY)
    smem = pl.BlockSpec(memory_space=pltpu.SMEM)
    bf16 = jnp.bfloat16
    dma = pltpu.SemaphoreType.DMA
    table = (-(-splits // 8) * 8, OUTPAD)
    return pl.pallas_call(
        functools.partial(kernel, n_blk, n_cset, half),
        out_shape=jax.ShapeDtypeStruct((n_cset * rows, width), bf16),
        in_specs=[smem] * 3 + [hbm] * 5,
        out_specs=hbm,
        scratch_shapes=[
            pltpu.VMEM((rows, channels), bf16),
            pltpu.VMEM((splits, sets), jnp.int32),
            pltpu.VMEM((splits, sets), jnp.int32),
            pltpu.VMEM(table, jnp.int32),
            pltpu.VMEM(table, jnp.int32),
            pltpu.VMEM((reach, slots, TILE, TILE), bf16),
            pltpu.VMEM((reach, rows, n_cset * rows), bf16),
            pltpu.VMEM((splits, rows, OUTPAD), bf16),
            pltpu.VMEM((splits, channels, OUTPAD), bf16),
            pltpu.VMEM((rows, channels), bf16),
            pltpu.VMEM((n_cset, rows, width), bf16),
        ]
        + [pltpu.VMEM((n_cset * rows, channels), bf16)] * (2 * half + 1)
        + [
            dma((5,)),
            dma((half + 1,)),
            dma((half + 1, n_cset)),
            dma((half, n_cset)),
            dma((half + 1, n_cset)),
            dma((half, n_cset)),
            dma((n_cset, pieces)),
            dma((n_cset, pieces)),
            dma((pieces,)),
        ],
        compiler_params=pltpu.CompilerParams(
            collective_id=0, has_side_effects=True, vmem_limit_bytes=56 * 1024 * 1024
        ),
    )(
        tile_dst[0, 0],
        tile_src[0, 0],
        tile_count[0, 0],
        active_table,
        passive_table,
        tiles,
        split_active,
        split_passive,
    )


def solution(mesh):
    in_specs = (
        P(("blk", "cset"), None),
        P(("blk", "cset"), None),
        P("blk", "cset", None, None, None, None),
        P("blk", "cset", None, None),
        P("blk", "cset", None, None),
        P("blk", "cset", None),
        P(),
        P(),
    )
    out_specs = P("blk", "cset")
    return jax.shard_map(local, mesh=mesh, in_specs=in_specs, out_specs=out_specs, check_vma=False)
```

time: 79.8 us -> 34.5 us (0.43)
  Pallas kernels: 0 us -> 31.1 us
  matrix products: 21.8 us -> 0 us
  blocking collectives: 19.8 us -> 0 us
  waiting for transfers between devices: 19.6 us -> 0 us
  local copies, waits for them, and re-layouts: 8.59 us -> 3.16 us
  starting transfers between devices: 4.83 us -> 0 us
  other arithmetic: 4.1 us -> 0 us
    pallas_call x0 -> x1, Pallas kernels: none -> 31.1 us  [local(): pl.pallas_call(functools.partial(kernel, n_blk, n_cset, half), out_shape=...]
    dot_general x50 -> x0, matrix products: 21.8 us -> none  [the longest x20 7.06 us: combine_sets(): jnp.dot(right, pick_right, preferred_element_type=jnp.float32)]
    all_gather x3 -> x0, blocking collectives: 19.8 us -> none  [the longest x1 7.48 us: local(): partition_rows = lax.all_gather(passive_table, 'cset', axis=0, tiled=True)]
    ppermute x4 -> x0, waiting for transfers between devices: 19.6 us -> none  [shifted(): return lax.ppermute(block, axis, route)]
    ppermute x4 -> x0, starting transfers between devices: 4.83 us -> none  [shifted(): return lax.ppermute(block, axis, route)]
    and x5 -> x0, other arithmetic: 3.85 us -> none  [add_partition(): chosen = jnp.take(blocks, src_rows, axis=0)]
    dynamic_slice x5 -> x0, local copies, waits for them, and re-layouts: 3.64 us -> none  [add_partition(): count_now = lax.dynamic_index_in_dim(count_all, slot, 0, keepdims=False)]
    unnamed x16 -> x2, local copies, waits for them, and re-layouts: 0.06 us -> 3.16 us
  transfers between devices with their start and end apart: 4 -> 0, of which waited for: 4 -> 0; matrix products, arithmetic and copies ran while one was open for 6% -> 0% of each run, Pallas kernels for 0% -> 0%
where the time goes in v1:
time: 34.5 us; the launch traced here: 34.2 us
  Pallas kernels  31.1 us (90%)
  local copies, waits for them, and re-layouts  3.16 us (9%)
    pallas_call x1, Pallas kernels, local(): pl.pallas_call(functools.partial(kernel, n_blk, n_cset, half), out_shape=...  31.1 us
    unnamed x2, local copies, waits for them, and re-layouts  3.16 us

profile of v1, /device:TPU:0, one launch (start us, length us, event | category | flops | bytes accessed | tf_op | source)
XLA Modules:
  0.0 34.2 jit_solution(10571587212926863506)
XLA Ops:
  0.0 1.3 %copy_bitcast_fusion = (s32[5,8]{1,0:T(8,128)}, s32[5,8]{1,0:T(8,128)}) fusion(s32[1,1,5,8]{3,1,2,0:T(1,128)} %param.12, s32[1,1,5,8]{3,1,2,0:T(1,128)} %param.11), kind=kLoop, calls=%fused_computation | loop fusion | bytes 640
  1.3 31.1 %shard_map.82 = bf16[512,512]{1,0:T(8,128)(2,1)} custom-call(s32[5,8]{1,0:T(8,128)} %get-tuple-element.6.dst_s, s32[5,8]{1,0:T(8,128)} %get-tuple-element.5.src_s, s32[5]{0:T(128)} %bitcast.7, bf16[256,256]{1,0:T(8,128)(2,1)} %active_h.1, bf16[256,256]{1,0:T(8,128)(2,1)} %passive_h.1, bf16[5,8,128,128]{3,2,1,0:T(8,128)(2,1)} %bitcast.6, s32[20,924]{1,0:T(8,128)} %left_h.1, ...), custom_call_target="tpu_custom_call" | custom-call | tf_op jit(solution)/shard_map/pallas_call | solution.py:249
  32.4 1.9 %copy.14 = bf16[512,512]{1,0:T(8,128)(2,1)} copy(bf16[512,512]{1,0:T(8,128)(2,1)} %shard_map.82) | data formatting | bytes 1048576

commit v2 on v1

--- a/solution.py
+++ b/solution.py
@@ -122,10 +122,10 @@
 
     copies[0].wait()
     copies[1].wait()
-    left_v[...] = jnp.full(left_v.shape, -1, jnp.int32)
-    right_v[...] = jnp.full(right_v.shape, -1, jnp.int32)
-    left_v[:splits, :sets] = left_raw[...]
-    right_v[:splits, :sets] = right_raw[...]
+    left_v[...] = jnp.full(left_v.shape, -1, jnp.float32)
+    right_v[...] = jnp.full(right_v.shape, -1, jnp.float32)
+    left_v[:splits, :sets] = left_raw[...].astype(jnp.float32)
+    right_v[:splits, :sets] = right_raw[...].astype(jnp.float32)
     copies[2].wait()
     copies[3].wait()
 
@@ -134,20 +134,25 @@
             for e in range(n_cset * rows // TILE):
                 total = jnp.zeros((TILE, TILE), jnp.bfloat16)
                 for t in range(tiles_v.shape[1]):
-                    here = (dst_s[r, t] == d) & (src_s[r, t] == e) & (count_s[r] > t)
+                    here = (dst_s[0, r, 0, t] == d) & (src_s[0, r, 0, t] == e) & (count_s[0, 0, r] > t)
                     total = total + jnp.where(here, tiles_v[r, t], jnp.zeros_like(total))
                 dense_v[r, d * TILE : (d + 1) * TILE, e * TILE : (e + 1) * TILE] = total
         return carry
 
-    channel = lax.broadcasted_iota(jnp.int32, (channels, 256), 0)
+    channel = lax.broadcasted_iota(jnp.int32, (channels, 256), 0).astype(jnp.bfloat16)
+    one, zero = jnp.ones(channel.shape, jnp.bfloat16), jnp.zeros(channel.shape, jnp.bfloat16)
+
+    def one_hot(table, j, columns):
+        row = jnp.broadcast_to(table[pl.ds(j, 1), columns], (16, 256)).astype(jnp.bfloat16)
+        return jnp.where(jnp.concatenate([row] * (channels // 16), axis=0) == channel, one, zero)
 
     def pick(j, carry):
         for at in range(0, OUTPAD, 256):
             columns = slice(at, at + 256)
-            left_one = (left_v[pl.ds(j, 1), columns] == channel).astype(jnp.bfloat16)
-            right_one = (right_v[pl.ds(j, 1), columns] == channel).astype(jnp.bfloat16)
-            choose_v[j, :, columns] = right_one
-            picked = jnp.dot(active_v[...], left_one, preferred_element_type=jnp.float32)
+            choose_v[j, :, columns] = one_hot(right_v, j, columns)
+            picked = jnp.dot(
+                active_v[...], one_hot(left_v, j, columns), preferred_element_type=jnp.float32
+            )
             picked_v[j, :, columns] = picked.astype(jnp.bfloat16)
         return carry
 
@@ -221,6 +226,17 @@
         for p in range(width // piece):
             block = out_h.at[part(other), pl.ds(p * piece, piece)]
             pltpu.make_async_copy(block, block, out_recv.at[other, p]).wait()
+
+
+def hand_over(joined_h, out_h, sem):
+    rows = out_h.shape[0] // 8
+    copies = []
+    for i in range(8):
+        block = pl.ds(i * rows, rows)
+        copies.append(pltpu.make_async_copy(joined_h.at[block, :], out_h.at[block, :], sem.at[i]))
+        copies[i].start()
+    for copy in copies:
+        copy.wait()
 
 
 def local(
@@ -246,7 +262,7 @@
     bf16 = jnp.bfloat16
     dma = pltpu.SemaphoreType.DMA
     table = (-(-splits // 8) * 8, OUTPAD)
-    return pl.pallas_call(
+    joined = pl.pallas_call(
         functools.partial(kernel, n_blk, n_cset, half),
         out_shape=jax.ShapeDtypeStruct((n_cset * rows, width), bf16),
         in_specs=[smem] * 3 + [hbm] * 5,
@@ -255,8 +271,8 @@
             pltpu.VMEM((rows, channels), bf16),
             pltpu.VMEM((splits, sets), jnp.int32),
             pltpu.VMEM((splits, sets), jnp.int32),
-            pltpu.VMEM(table, jnp.int32),
-            pltpu.VMEM(table, jnp.int32),
+            pltpu.VMEM(table, jnp.float32),
+            pltpu.VMEM(table, jnp.float32),
             pltpu.VMEM((reach, slots, TILE, TILE), bf16),
             pltpu.VMEM((reach, rows, n_cset * rows), bf16),
             pltpu.VMEM((splits, rows, OUTPAD), bf16),
@@ -280,15 +296,23 @@
             collective_id=0, has_side_effects=True, vmem_limit_bytes=56 * 1024 * 1024
         ),
     )(
-        tile_dst[0, 0],
-        tile_src[0, 0],
-        tile_count[0, 0],
+        jnp.transpose(tile_dst, (0, 2, 1, 3)),
+        jnp.transpose(tile_src, (0, 2, 1, 3)),
+        tile_count,
         active_table,
         passive_table,
         tiles,
         split_active,
         split_passive,
     )
+    return pl.pallas_call(
+        hand_over,
+        out_shape=joined,
+        in_specs=[hbm],
+        out_specs=hbm,
+        scratch_shapes=[dma((8,))],
+        compiler_params=pltpu.CompilerParams(vmem_limit_bytes=56 * 1024 * 1024),
+    )(joined)
 
 
 def solution(mesh):

time: 34.5 us -> 46.8 us (1.36)
  Pallas kernels: 31.1 us -> 46.6 us
  local copies, waits for them, and re-layouts: 3.16 us -> 0 us
    pallas_call x0 -> x1, Pallas kernels: none -> 17.1 us  [local(): pl.pallas_call(hand_over, out_shape=joined, in_specs=[hbm], out_specs=hbm...]
    unnamed x2 -> x0, local copies, waits for them, and re-layouts: 3.16 us -> none
    pallas_call x1, Pallas kernels: 31.1 us -> 29.6 us  [local(): pl.pallas_call(functools.partial(kernel, n_blk, n_cset, half), out_shape=...]
where the time goes in v2:
time: 46.8 us; the launch traced here: 46.6 us
  Pallas kernels  46.6 us (100%)
    pallas_call x1, Pallas kernels, local(): pl.pallas_call(functools.partial(kernel, n_blk, n_cset, half), out_shape=...  29.6 us
    pallas_call x1, Pallas kernels, local(): pl.pallas_call(hand_over, out_shape=joined, in_specs=[hbm], out_specs=hbm...  17.1 us

profile of v2, /device:TPU:0, one launch (start us, length us, event | category | flops | bytes accessed | tf_op | source)
XLA Modules:
  0.0 46.6 jit_solution(13943617837081402913)
XLA Ops:
  0.0 29.6 %shard_map.82.joined_h = bf16[512,512]{1,0:T(8,128)(2,1)} custom-call(s32[1,5,1,8]{3,2,1,0:T(1,128)} %bitcast.4, s32[1,5,1,8]{3,2,1,0:T(1,128)} %bitcast.5, s32[1,1,5]{2,1,0:T(1,128)} %count_s.1, bf16[256,256]{1,0:T(8,128)(2,1)} %active_h.1, bf16[256,256]{1,0:T(8,128)(2,1)} %passive_h.1, bf16[5,8,128,128]{3,2,1,0:T(8,128)(2,1)} %bitcast.3, ...), custom_call_target="tpu_custom_call" | custom-call | tf_op jit(solution)/shard_map/pallas_call | solution.py:265
  29.6 17.1 %shard_map.83 = bf16[512,512]{1,0:T(8,128)(2,1)} custom-call(bf16[512,512]{1,0:T(8,128)(2,1)} %shard_map.82.joined_h), custom_call_target="tpu_custom_call" | custom-call | tf_op jit(solution)/shard_map/pallas_call | solution.py:308

commit v3 on v2

--- a/solution.py
+++ b/solution.py
@@ -9,6 +9,7 @@
 
 OUTPAD = 1024
 TILE = 128
+CHUNKS = 4
 MESH = pl.DeviceIdType.MESH
 
 
@@ -24,7 +25,7 @@
     adjacency_h,
     left_h,
     right_h,
-    out_h,
+    out_ref,
     active_v,
     left_raw,
     right_raw,
@@ -49,13 +50,12 @@
         away_recv,
         out_send,
         out_recv,
-        out_local,
     ) = rest[2 * half + 1 :]
     b = lax.axis_index("blk")
     c = lax.axis_index("cset")
     rows, channels = active_v.shape
     splits, sets = left_raw.shape
-    width = out_h.shape[1]
+    width = out_ref.shape[1]
     piece = min(width, 256)
     sign = 2 * (b % 2) - 1
     sibling = (b - sign, c)
@@ -82,10 +82,10 @@
         copy.start()
     pl.semaphore_wait(barrier, len(senders))
 
-    started = []
-
-    def part(cset):
-        return pl.ds(pl.multiple_of(cset * rows, rows), rows)
+    size = rows // CHUNKS
+
+    def part(cset, q=0, length=size):
+        return pl.ds(pl.multiple_of(cset * rows + q * size, size), length)
 
     def send(src, dst, send_sem, recv_sem, device):
         copy = pltpu.make_async_remote_copy(
@@ -97,28 +97,36 @@
             device_id_type=MESH,
         )
         copy.start()
-        started.append(copy)
-
-    def to_others(block, k):
+
+    def to_others(k, q):
+        block = home[k].at[part(c, q), :]
         for i, other in enumerate(others):
-            send(block, home[k].at[mine, :], side_send.at[k, i], home_recv.at[k, c], (b, other))
-
-    def to_sibling(block, k, cset):
+            send(block, block, side_send.at[k, i, q], home_recv.at[k, c, q], (b, other))
+
+    def to_sibling(k, cset, q):
         send(
-            block,
-            away[k + 1].at[part(cset), :],
-            sibling_send.at[k, cset],
-            away_recv.at[k, cset],
+            home[k].at[part(cset, q), :],
+            away[k + 1].at[part(cset, q), :],
+            sibling_send.at[k, cset, q],
+            away_recv.at[k, cset, q],
             sibling,
         )
 
-    def arrived(ref, cset, sem):
-        pltpu.make_async_copy(ref.at[part(cset), :], ref.at[part(cset), :], sem).wait()
-
-    for k in range(half, 0, -1):
-        send(passive_h, home[k].at[mine, :], own_send.at[k], home_recv.at[k, c], targets[k])
-    to_others(passive_h, 0)
-    to_sibling(passive_h, 0, c)
+    def arrived(ref, cset, q, sem):
+        block = ref.at[part(cset, q), :]
+        pltpu.make_async_copy(block, block, sem).wait()
+
+    copies[4].wait()
+    def begin(q, carry):
+        block = home[0].at[part(c, q), :]
+        for k in range(half, 0, -1):
+            goal = home[k].at[part(c, q), :]
+            send(block, goal, own_send.at[k - 1, q], home_recv.at[k, c, q], targets[k])
+        to_others(0, q)
+        to_sibling(0, c, q)
+        return carry
+
+    lax.fori_loop(0, CHUNKS, begin, 0)
 
     copies[0].wait()
     copies[1].wait()
@@ -146,7 +154,7 @@
         row = jnp.broadcast_to(table[pl.ds(j, 1), columns], (16, 256)).astype(jnp.bfloat16)
         return jnp.where(jnp.concatenate([row] * (channels // 16), axis=0) == channel, one, zero)
 
-    def pick(j, carry):
+    def pick(j):
         for at in range(0, OUTPAD, 256):
             columns = slice(at, at + 256)
             choose_v[j, :, columns] = one_hot(right_v, j, columns)
@@ -154,48 +162,62 @@
                 active_v[...], one_hot(left_v, j, columns), preferred_element_type=jnp.float32
             )
             picked_v[j, :, columns] = picked.astype(jnp.bfloat16)
-        return carry
-
-    def side_arrived(k):
+
+    def side_arrived(k, q):
         for other in others:
-            arrived(home[k], other, home_recv.at[k, other])
+            arrived(home[k], other, q, home_recv.at[k, other, q])
             if k < half:
-                to_sibling(home[k].at[part(other), :], k, other)
-
-    def own_arrived(k):
-        arrived(home[k], c, home_recv.at[k, c])
-        to_others(home[k].at[mine, :], k)
+                to_sibling(k, other, q)
+
+    def own_arrived(k, q):
+        arrived(home[k], c, q, home_recv.at[k, c, q])
+        to_others(k, q)
         if k < half:
-            to_sibling(home[k].at[mine, :], k, c)
-
-    stages = [functools.partial(own_arrived, 1), functools.partial(side_arrived, 0)]
-    for k in range(2, half + 1):
-        stages += [functools.partial(own_arrived, k), functools.partial(side_arrived, k - 1)]
+            to_sibling(k, c, q)
+
+    lead = CHUNKS * (half + 1)
+    stages = lead + CHUNKS * (half - 1)
+    first = max(splits - stages, 0)
+
+    def advance(j, carry):
+        pl.when(j < splits)(lambda: pick(j))
+        i = j - first
+        for k in range(1, half + 1):
+            now = (i >= 0) & (i < lead) & (i % (half + 1) == k - 1)
+            pl.when(now)(functools.partial(own_arrived, k, i // (half + 1)))
+        now = (i >= 0) & (i < lead) & (i % (half + 1) == half)
+        pl.when(now)(functools.partial(side_arrived, 0, i // (half + 1)))
+        for k in range(1, half):
+            start = lead + CHUNKS * (k - 1)
+            now = (i >= start) & (i < start + CHUNKS)
+            pl.when(now)(functools.partial(side_arrived, k, i - start))
+        return carry
 
     lax.fori_loop(0, 2 * half + 1, assemble, 0)
-    for i, stage in enumerate(stages):
-        lax.fori_loop(splits * i // len(stages), splits * (i + 1) // len(stages), pick, 0)
-        stage()
+    lax.fori_loop(0, first + stages, advance, 0)
 
     def times(r, ref):
         return jnp.dot(dense_v[r], ref[...], preferred_element_type=jnp.float32)
 
-    copies[4].wait()
     total = times(half, home[0])
     for k in range(1, half):
         total = total + times(half + sign * k, home[k])
     for k in range(1, half + 1):
         for cset in [c] + others:
-            arrived(away[k], cset, away_recv.at[k - 1, cset])
+            for q in range(CHUNKS):
+                arrived(away[k], cset, q, away_recv.at[k - 1, cset, q])
         total = total + times(half - sign * k, away[k])
-    side_arrived(half)
+    for q in range(CHUNKS):
+        side_arrived(half, q)
     total = total + times(half + sign * half, home[half])
     neighbour_v[...] = total.astype(jnp.bfloat16)
 
-    results = []
+    pieces = width // piece
     for i, owner in enumerate(others + [c]):
-        for p in range(width // piece):
+
+        def join(p, carry):
             columns = pl.ds(pl.multiple_of(owner * width + p * piece, piece), piece)
+            inside = pl.ds(pl.multiple_of(p * piece, piece), piece)
 
             def step(g, total):
                 for u in range(4):
@@ -209,34 +231,41 @@
                 return total
 
             total = lax.fori_loop(0, splits // 4, step, jnp.zeros((rows, piece), jnp.float32))
-            result_v[i, :, p * piece : (p + 1) * piece] = total.astype(jnp.bfloat16)
-            block = result_v.at[i, :, pl.ds(p * piece, piece)]
-            goal = out_h.at[mine, pl.ds(p * piece, piece)]
             if i < n_cset - 1:
-                send(block, goal, out_send.at[i, p], out_recv.at[c, p], (b, owner))
+                result_v[i, :, inside] = total.astype(jnp.bfloat16)
+                send(
+                    result_v.at[i, :, inside],
+                    out_ref.at[part(c, 0, rows), inside],
+                    out_send.at[i, p],
+                    out_recv.at[c, p],
+                    (b, owner),
+                )
             else:
-                copy = pltpu.make_async_copy(block, goal, out_local.at[p])
-                copy.start()
-                results.append(copy)
-    for copy in results:
-        copy.wait()
-    for copy in started:
-        copy.wait_send()
-    for other in others:
-        for p in range(width // piece):
-            block = out_h.at[part(other), pl.ds(p * piece, piece)]
+                out_ref[part(c, 0, rows), inside] = total.astype(jnp.bfloat16)
+            return carry
+
+        lax.fori_loop(0, pieces, join, 0)
+
+    def finish(q, carry):
+        block = home[0].at[part(c, q), :]
+        sems = [own_send.at[k, q] for k in range(half)]
+        sems += [side_send.at[k, i, q] for k in range(half + 1) for i in range(n_cset - 1)]
+        sems += [sibling_send.at[k, i, q] for k in range(half) for i in range(n_cset)]
+        for sem in sems:
+            pltpu.make_async_copy(block, block, sem).wait()
+        return carry
+
+    def finish_out(p, carry):
+        inside = pl.ds(pl.multiple_of(p * piece, piece), piece)
+        for i, other in enumerate(others):
+            block = result_v.at[i, :, inside]
+            pltpu.make_async_copy(block, block, out_send.at[i, p]).wait()
+            block = out_ref.at[part(other, 0, rows), inside]
             pltpu.make_async_copy(block, block, out_recv.at[other, p]).wait()
-
-
-def hand_over(joined_h, out_h, sem):
-    rows = out_h.shape[0] // 8
-    copies = []
-    for i in range(8):
-        block = pl.ds(i * rows, rows)
-        copies.append(pltpu.make_async_copy(joined_h.at[block, :], out_h.at[block, :], sem.at[i]))
-        copies[i].start()
-    for copy in copies:
-        copy.wait()
+        return carry
+
+    lax.fori_loop(0, CHUNKS, finish, 0)
+    lax.fori_loop(0, pieces, finish_out, 0)
 
 
 def local(
@@ -262,11 +291,11 @@
     bf16 = jnp.bfloat16
     dma = pltpu.SemaphoreType.DMA
     table = (-(-splits // 8) * 8, OUTPAD)
-    joined = pl.pallas_call(
+    return pl.pallas_call(
         functools.partial(kernel, n_blk, n_cset, half),
-        out_shape=jax.ShapeDtypeStruct((n_cset * rows, width), bf16),
+        out_shape=pltpu.VMEM((n_cset * rows, width), bf16),
         in_specs=[smem] * 3 + [hbm] * 5,
-        out_specs=hbm,
+        out_specs=pl.BlockSpec(memory_space=pltpu.VMEM),
         scratch_shapes=[
             pltpu.VMEM((rows, channels), bf16),
             pltpu.VMEM((splits, sets), jnp.int32),
@@ -278,19 +307,18 @@
             pltpu.VMEM((splits, rows, OUTPAD), bf16),
             pltpu.VMEM((splits, channels, OUTPAD), bf16),
             pltpu.VMEM((rows, channels), bf16),
-            pltpu.VMEM((n_cset, rows, width), bf16),
+            pltpu.VMEM((max(n_cset - 1, 1), rows, width), bf16),
         ]
         + [pltpu.VMEM((n_cset * rows, channels), bf16)] * (2 * half + 1)
         + [
             dma((5,)),
-            dma((half + 1,)),
-            dma((half + 1, n_cset)),
-            dma((half, n_cset)),
-            dma((half + 1, n_cset)),
-            dma((half, n_cset)),
+            dma((half, CHUNKS)),
+            dma((half + 1, n_cset, CHUNKS)),
+            dma((half, n_cset, CHUNKS)),
+            dma((half + 1, n_cset, CHUNKS)),
+            dma((half, n_cset, CHUNKS)),
             dma((n_cset, pieces)),
             dma((n_cset, pieces)),
-            dma((pieces,)),
         ],
         compiler_params=pltpu.CompilerParams(
             collective_id=0, has_side_effects=True, vmem_limit_bytes=56 * 1024 * 1024
@@ -305,14 +333,6 @@
         split_active,
         split_passive,
     )
-    return pl.pallas_call(
-        hand_over,
-        out_shape=joined,
-        in_specs=[hbm],
-        out_specs=hbm,
-        scratch_shapes=[dma((8,))],
-        compiler_params=pltpu.CompilerParams(vmem_limit_bytes=56 * 1024 * 1024),
-    )(joined)
 
 
 def solution(mesh):

time: 46.8 us -> 30.2 us (0.65)
  Pallas kernels: 46.6 us -> 29.2 us
  local copies, waits for them, and re-layouts: 0 us -> 0.8 us
    pallas_call x1 -> x0, Pallas kernels: 17.1 us -> none  [local(): pl.pallas_call(hand_over, out_shape=joined, in_specs=[hbm], out_specs=hbm...]
    unnamed x0 -> x1, local copies, waits for them, and re-layouts: none -> 0.8 us
where the time goes in v3:
time: 30.2 us; the launch traced here: 30 us
  Pallas kernels  29.2 us (97%)
  local copies, waits for them, and re-layouts  0.8 us (3%)
    pallas_call x1, Pallas kernels, local(): pl.pallas_call(functools.partial(kernel, n_blk, n_cset, half), out_shape=...  29.2 us
    unnamed x1, local copies, waits for them, and re-layouts  0.8 us

profile of v3, /device:TPU:0, one launch (start us, length us, event | category | flops | bytes accessed | tf_op | source)
XLA Modules:
  0.0 30.0 jit_solution(5037627247453342504)
XLA Ops:
  0.0 29.2 %shard_map.82 = bf16[512,512]{1,0:T(8,128)(2,1)S(1)} custom-call(s32[1,5,1,8]{3,2,1,0:T(1,128)} %bitcast.4, s32[1,5,1,8]{3,2,1,0:T(1,128)} %bitcast.5, s32[1,1,5]{2,1,0:T(1,128)} %count_s.1, bf16[256,256]{1,0:T(8,128)(2,1)} %active_h.1, bf16[256,256]{1,0:T(8,128)(2,1)} %passive_h.1, bf16[5,8,128,128]{3,2,1,0:T(8,128)(2,1)} %bitcast.3, s32[20,924]{1,0:T(8,128)} %left_h.1, ...), custom_call_target="tpu_custom_call" | custom-call | tf_op jit(solution)/shard_map/pallas_call | solution.py:294
  29.2 0.8 %copy.10 = bf16[512,512]{1,0:T(8,128)(2,1)} copy(bf16[512,512]{1,0:T(8,128)(2,1)S(1)} %shard_map.82) | data formatting | bytes 1048576

commit v4 on v3

--- a/solution.py
+++ b/solution.py
@@ -10,6 +10,7 @@
 OUTPAD = 1024
 TILE = 128
 CHUNKS = 4
+GROUP = 4
 MESH = pl.DeviceIdType.MESH
 
 
@@ -137,7 +138,7 @@
     copies[2].wait()
     copies[3].wait()
 
-    def assemble(r, carry):
+    def assemble(r):
         for d in range(rows // TILE):
             for e in range(n_cset * rows // TILE):
                 total = jnp.zeros((TILE, TILE), jnp.bfloat16)
@@ -145,7 +146,6 @@
                     here = (dst_s[0, r, 0, t] == d) & (src_s[0, r, 0, t] == e) & (count_s[0, 0, r] > t)
                     total = total + jnp.where(here, tiles_v[r, t], jnp.zeros_like(total))
                 dense_v[r, d * TILE : (d + 1) * TILE, e * TILE : (e + 1) * TILE] = total
-        return carry
 
     channel = lax.broadcasted_iota(jnp.int32, (channels, 256), 0).astype(jnp.bfloat16)
     one, zero = jnp.ones(channel.shape, jnp.bfloat16), jnp.zeros(channel.shape, jnp.bfloat16)
@@ -154,14 +154,17 @@
         row = jnp.broadcast_to(table[pl.ds(j, 1), columns], (16, 256)).astype(jnp.bfloat16)
         return jnp.where(jnp.concatenate([row] * (channels // 16), axis=0) == channel, one, zero)
 
-    def pick(j):
-        for at in range(0, OUTPAD, 256):
-            columns = slice(at, at + 256)
-            choose_v[j, :, columns] = one_hot(right_v, j, columns)
-            picked = jnp.dot(
-                active_v[...], one_hot(left_v, j, columns), preferred_element_type=jnp.float32
-            )
-            picked_v[j, :, columns] = picked.astype(jnp.bfloat16)
+    def pick(start):
+        for j in range(GROUP):
+            for at in range(0, OUTPAD, 256):
+                columns = slice(at, at + 256)
+                choose_v[start + j, :, columns] = one_hot(right_v, start + j, columns)
+                picked = jnp.dot(
+                    active_v[...],
+                    one_hot(left_v, start + j, columns),
+                    preferred_element_type=jnp.float32,
+                )
+                picked_v[start + j, :, columns] = picked.astype(jnp.bfloat16)
 
     def side_arrived(k, q):
         for other in others:
@@ -175,26 +178,29 @@
         if k < half:
             to_sibling(k, c, q)
 
-    lead = CHUNKS * (half + 1)
-    stages = lead + CHUNKS * (half - 1)
-    first = max(splits - stages, 0)
-
-    def advance(j, carry):
-        pl.when(j < splits)(lambda: pick(j))
-        i = j - first
-        for k in range(1, half + 1):
-            now = (i >= 0) & (i < lead) & (i % (half + 1) == k - 1)
-            pl.when(now)(functools.partial(own_arrived, k, i // (half + 1)))
-        now = (i >= 0) & (i < lead) & (i % (half + 1) == half)
-        pl.when(now)(functools.partial(side_arrived, 0, i // (half + 1)))
+    groups = splits // GROUP
+    reach = 2 * half + 1
+
+    def advance(g, carry):
+        pl.when(g < groups)(functools.partial(pick, g * GROUP))
+        pl.when(g < reach)(functools.partial(assemble, g))
+
+        @pl.when((g >= 1) & (g <= CHUNKS))
+        def _():
+            for k in range(1, half + 1):
+                own_arrived(k, g - 1)
+            side_arrived(0, g - 1)
+
+        return carry
+
+    lax.fori_loop(0, max(groups, reach, CHUNKS + 1), advance, 0)
+
+    def forward(q, carry):
         for k in range(1, half):
-            start = lead + CHUNKS * (k - 1)
-            now = (i >= start) & (i < start + CHUNKS)
-            pl.when(now)(functools.partial(side_arrived, k, i - start))
-        return carry
-
-    lax.fori_loop(0, 2 * half + 1, assemble, 0)
-    lax.fori_loop(0, first + stages, advance, 0)
+            side_arrived(k, q)
+        return carry
+
+    lax.fori_loop(0, CHUNKS, forward, 0)
 
     def times(r, ref):
         return jnp.dot(dense_v[r], ref[...], preferred_element_type=jnp.float32)
@@ -213,38 +219,37 @@
     neighbour_v[...] = total.astype(jnp.bfloat16)
 
     pieces = width // piece
-    for i, owner in enumerate(others + [c]):
-
-        def join(p, carry):
-            columns = pl.ds(pl.multiple_of(owner * width + p * piece, piece), piece)
-            inside = pl.ds(pl.multiple_of(p * piece, piece), piece)
-
-            def step(g, total):
-                for u in range(4):
-                    j = g * 4 + u
-                    found = jnp.dot(
-                        neighbour_v[...],
-                        choose_v[j, :, columns],
-                        preferred_element_type=jnp.float32,
-                    )
-                    total = total + picked_v[j, :, columns].astype(jnp.float32) * found
-                return total
-
-            total = lax.fori_loop(0, splits // 4, step, jnp.zeros((rows, piece), jnp.float32))
-            if i < n_cset - 1:
-                result_v[i, :, inside] = total.astype(jnp.bfloat16)
-                send(
-                    result_v.at[i, :, inside],
-                    out_ref.at[part(c, 0, rows), inside],
-                    out_send.at[i, p],
-                    out_recv.at[c, p],
-                    (b, owner),
-                )
-            else:
-                out_ref[part(c, 0, rows), inside] = total.astype(jnp.bfloat16)
-            return carry
-
-        lax.fori_loop(0, pieces, join, 0)
+
+    def join(n, carry):
+        i, p = n // pieces, n % pieces
+        owner = (c + 1 + i) % n_cset
+        columns = pl.ds(pl.multiple_of(owner * width + p * piece, piece), piece)
+        inside = pl.ds(pl.multiple_of(p * piece, piece), piece)
+        total = jnp.zeros((rows, piece), jnp.float32)
+        for j in range(splits):
+            found = jnp.dot(
+                neighbour_v[...], choose_v[j, :, columns], preferred_element_type=jnp.float32
+            )
+            total = total + picked_v[j, :, columns].astype(jnp.float32) * found
+        result_v[i, :, inside] = total.astype(jnp.bfloat16)
+
+        @pl.when(i < n_cset - 1)
+        def _():
+            send(
+                result_v.at[i, :, inside],
+                out_ref.at[part(c, 0, rows), inside],
+                out_send.at[i, p],
+                out_recv.at[c, p],
+                (b, owner),
+            )
+
+        @pl.when(i == n_cset - 1)
+        def _():
+            out_ref[part(c, 0, rows), inside] = result_v[i, :, inside]
+
+        return carry
+
+    lax.fori_loop(0, n_cset * pieces, join, 0)
 
     def finish(q, carry):
         block = home[0].at[part(c, q), :]
@@ -307,7 +312,7 @@
             pltpu.VMEM((splits, rows, OUTPAD), bf16),
             pltpu.VMEM((splits, channels, OUTPAD), bf16),
             pltpu.VMEM((rows, channels), bf16),
-            pltpu.VMEM((max(n_cset - 1, 1), rows, width), bf16),
+            pltpu.VMEM((n_cset, rows, width), bf16),
         ]
         + [pltpu.VMEM((n_cset * rows, channels), bf16)] * (2 * half + 1)
         + [

time: 30.2 us -> 29.2 us (0.967)
  Pallas kernels: 29.2 us -> 28.3 us
    pallas_call x1, Pallas kernels: 29.2 us -> 28.3 us  [local(): pl.pallas_call(functools.partial(kernel, n_blk, n_cset, half), out_shape=...]
where the time goes in v4:
time: 29.2 us; the launch traced here: 29.1 us
  Pallas kernels  28.3 us (97%)
  local copies, waits for them, and re-layouts  0.8 us (3%)
    pallas_call x1, Pallas kernels, local(): pl.pallas_call(functools.partial(kernel, n_blk, n_cset, half), out_shape=...  28.3 us
    unnamed x1, local copies, waits for them, and re-layouts  0.8 us

profile of v4, /device:TPU:0, one launch (start us, length us, event | category | flops | bytes accessed | tf_op | source)
XLA Modules:
  0.0 29.1 jit_solution(1093075104763921664)
XLA Ops:
  0.0 28.3 %shard_map.82 = bf16[512,512]{1,0:T(8,128)(2,1)S(1)} custom-call(s32[1,5,1,8]{3,2,1,0:T(1,128)} %bitcast.4, s32[1,5,1,8]{3,2,1,0:T(1,128)} %bitcast.5, s32[1,1,5]{2,1,0:T(1,128)} %count_s.1, bf16[256,256]{1,0:T(8,128)(2,1)} %active_h.1, bf16[256,256]{1,0:T(8,128)(2,1)} %passive_h.1, bf16[5,8,128,128]{3,2,1,0:T(8,128)(2,1)} %bitcast.3, s32[20,924]{1,0:T(8,128)} %left_h.1, ...), custom_call_target="tpu_custom_call" | custom-call | tf_op jit(solution)/shard_map/pallas_call | solution.py:299
  28.3 0.8 %copy.10 = bf16[512,512]{1,0:T(8,128)(2,1)} copy(bf16[512,512]{1,0:T(8,128)(2,1)S(1)} %shard_map.82) | data formatting | bytes 1048576

commit v5 on v4

--- a/solution.py
+++ b/solution.py
@@ -32,12 +32,14 @@
     right_raw,
     left_v,
     right_v,
+    left_own,
+    right_own,
     tiles_v,
     dense_v,
     picked_v,
-    choose_v,
+    choose_left_v,
+    choose_right_v,
     neighbour_v,
-    result_v,
     *rest,
 ):
     home = rest[: half + 1]
@@ -49,12 +51,16 @@
         sibling_send,
         home_recv,
         away_recv,
-        out_send,
-        out_recv,
+        far_send,
+        active_send,
+        active_recv,
+        sum_send,
+        sum_recv,
     ) = rest[2 * half + 1 :]
     b = lax.axis_index("blk")
     c = lax.axis_index("cset")
-    rows, channels = active_v.shape
+    channels = active_v.shape[1]
+    rows = active_v.shape[0] // n_cset
     splits, sets = left_raw.shape
     width = out_ref.shape[1]
     piece = min(width, 256)
@@ -75,7 +81,7 @@
     copies = [
         pltpu.make_async_copy(left_h, left_raw, local_sem.at[0]),
         pltpu.make_async_copy(right_h, right_raw, local_sem.at[1]),
-        pltpu.make_async_copy(active_h, active_v, local_sem.at[2]),
+        pltpu.make_async_copy(active_h, active_v.at[mine, :], local_sem.at[2]),
         pltpu.make_async_copy(adjacency_h, tiles_v, local_sem.at[3]),
         pltpu.make_async_copy(passive_h, home[0].at[mine, :], local_sem.at[4]),
     ]
@@ -135,6 +141,9 @@
     right_v[...] = jnp.full(right_v.shape, -1, jnp.float32)
     left_v[:splits, :sets] = left_raw[...].astype(jnp.float32)
     right_v[:splits, :sets] = right_raw[...].astype(jnp.float32)
+    own_columns = pl.ds(pl.multiple_of(c * width, width), width)
+    left_own[...] = left_v[:, own_columns]
+    right_own[...] = right_v[:, own_columns]
     copies[2].wait()
     copies[3].wait()
 
@@ -147,35 +156,54 @@
                     total = total + jnp.where(here, tiles_v[r, t], jnp.zeros_like(total))
                 dense_v[r, d * TILE : (d + 1) * TILE, e * TILE : (e + 1) * TILE] = total
 
-    channel = lax.broadcasted_iota(jnp.int32, (channels, 256), 0).astype(jnp.bfloat16)
+    channel = lax.broadcasted_iota(jnp.int32, (channels, piece), 0).astype(jnp.bfloat16)
     one, zero = jnp.ones(channel.shape, jnp.bfloat16), jnp.zeros(channel.shape, jnp.bfloat16)
 
     def one_hot(table, j, columns):
-        row = jnp.broadcast_to(table[pl.ds(j, 1), columns], (16, 256)).astype(jnp.bfloat16)
+        row = jnp.broadcast_to(table[pl.ds(j, 1), columns], (16, piece)).astype(jnp.bfloat16)
         return jnp.where(jnp.concatenate([row] * (channels // 16), axis=0) == channel, one, zero)
 
     def pick(start):
         for j in range(GROUP):
-            for at in range(0, OUTPAD, 256):
-                columns = slice(at, at + 256)
-                choose_v[start + j, :, columns] = one_hot(right_v, start + j, columns)
-                picked = jnp.dot(
-                    active_v[...],
-                    one_hot(left_v, start + j, columns),
-                    preferred_element_type=jnp.float32,
-                )
-                picked_v[start + j, :, columns] = picked.astype(jnp.bfloat16)
+            for at in range(0, width, piece):
+                inside = slice(at, at + piece)
+                left = one_hot(left_own, start + j, inside)
+                choose_left_v[start + j, :, inside] = left
+                choose_right_v[start + j, :, inside] = one_hot(right_own, start + j, inside)
+                picked = jnp.dot(active_v[mine, :], left, preferred_element_type=jnp.float32)
+                picked_v[start + j, mine, inside] = picked.astype(jnp.bfloat16)
+
+    def pick_others(start):
+        for other in others:
+            there = part(other, 0, rows)
+            for j in range(GROUP):
+                for at in range(0, width, piece):
+                    inside = slice(at, at + piece)
+                    picked = jnp.dot(
+                        active_v[there, :],
+                        choose_left_v[start + j, :, inside],
+                        preferred_element_type=jnp.float32,
+                    )
+                    picked_v[start + j, there, inside] = picked.astype(jnp.bfloat16)
 
     def side_arrived(k, q):
         for other in others:
             arrived(home[k], other, q, home_recv.at[k, other, q])
+            if k == 0:
+                send(
+                    home[0].at[part(other, q), :],
+                    home[half].at[part(other, q), :],
+                    far_send.at[other, q],
+                    home_recv.at[half, other, q],
+                    targets[half],
+                )
             if k < half:
                 to_sibling(k, other, q)
 
     def own_arrived(k, q):
         arrived(home[k], c, q, home_recv.at[k, c, q])
-        to_others(k, q)
         if k < half:
+            to_others(k, q)
             to_sibling(k, c, q)
 
     groups = splits // GROUP
@@ -183,24 +211,38 @@
 
     def advance(g, carry):
         pl.when(g < groups)(functools.partial(pick, g * GROUP))
-        pl.when(g < reach)(functools.partial(assemble, g))
 
         @pl.when((g >= 1) & (g <= CHUNKS))
         def _():
+            side_arrived(0, g - 1)
             for k in range(1, half + 1):
                 own_arrived(k, g - 1)
-            side_arrived(0, g - 1)
-
+
+        @pl.when(g == 1)
+        def _():
+            for i, other in enumerate(others):
+                block = active_v.at[mine, :]
+                send(block, block, active_send.at[i], active_recv.at[c], (b, other))
+
+        pl.when(g < reach)(functools.partial(assemble, g))
         return carry
 
     lax.fori_loop(0, max(groups, reach, CHUNKS + 1), advance, 0)
-
-    def forward(q, carry):
-        for k in range(1, half):
-            side_arrived(k, q)
-        return carry
-
-    lax.fori_loop(0, CHUNKS, forward, 0)
+    for other in others:
+        block = active_v.at[part(other, 0, rows), :]
+        pltpu.make_async_copy(block, block, active_recv.at[other]).wait()
+
+    def forward(g, carry):
+        pl.when(g < groups)(functools.partial(pick_others, g * GROUP))
+
+        @pl.when(g < CHUNKS)
+        def _():
+            for k in range(1, half):
+                side_arrived(k, g)
+
+        return carry
+
+    lax.fori_loop(0, max(groups, CHUNKS), forward, 0)
 
     def times(r, ref):
         return jnp.dot(dense_v[r], ref[...], preferred_element_type=jnp.float32)
@@ -216,37 +258,32 @@
     for q in range(CHUNKS):
         side_arrived(half, q)
     total = total + times(half + sign * half, home[half])
-    neighbour_v[...] = total.astype(jnp.bfloat16)
-
+    neighbour_v[mine, :] = total.astype(jnp.bfloat16)
+    for i, other in enumerate(others):
+        block = neighbour_v.at[mine, :]
+        send(block, block, sum_send.at[i], sum_recv.at[c], (b, other))
     pieces = width // piece
 
     def join(n, carry):
         i, p = n // pieces, n % pieces
-        owner = (c + 1 + i) % n_cset
-        columns = pl.ds(pl.multiple_of(owner * width + p * piece, piece), piece)
+        owner = (c + i) % n_cset
+        there = part(owner, 0, rows)
         inside = pl.ds(pl.multiple_of(p * piece, piece), piece)
+
+        @pl.when((i > 0) & (p == 0))
+        def _():
+            block = neighbour_v.at[there, :]
+            pltpu.make_async_copy(block, block, sum_recv.at[owner]).wait()
+
         total = jnp.zeros((rows, piece), jnp.float32)
         for j in range(splits):
             found = jnp.dot(
-                neighbour_v[...], choose_v[j, :, columns], preferred_element_type=jnp.float32
+                neighbour_v[there, :],
+                choose_right_v[j, :, inside],
+                preferred_element_type=jnp.float32,
             )
-            total = total + picked_v[j, :, columns].astype(jnp.float32) * found
-        result_v[i, :, inside] = total.astype(jnp.bfloat16)
-
-        @pl.when(i < n_cset - 1)
-        def _():
-            send(
-                result_v.at[i, :, inside],
-                out_ref.at[part(c, 0, rows), inside],
-                out_send.at[i, p],
-                out_recv.at[c, p],
-                (b, owner),
-            )
-
-        @pl.when(i == n_cset - 1)
-        def _():
-            out_ref[part(c, 0, rows), inside] = result_v[i, :, inside]
-
+            total = total + picked_v[j, there, inside].astype(jnp.float32) * found
+        out_ref[there, inside] = total.astype(jnp.bfloat16)
         return carry
 
     lax.fori_loop(0, n_cset * pieces, join, 0)
@@ -254,23 +291,19 @@
     def finish(q, carry):
         block = home[0].at[part(c, q), :]
         sems = [own_send.at[k, q] for k in range(half)]
-        sems += [side_send.at[k, i, q] for k in range(half + 1) for i in range(n_cset - 1)]
+        sems += [side_send.at[k, i, q] for k in range(half) for i in range(n_cset - 1)]
         sems += [sibling_send.at[k, i, q] for k in range(half) for i in range(n_cset)]
+        sems += [far_send.at[other, q] for other in others]
         for sem in sems:
             pltpu.make_async_copy(block, block, sem).wait()
         return carry
 
-    def finish_out(p, carry):
-        inside = pl.ds(pl.multiple_of(p * piece, piece), piece)
-        for i, other in enumerate(others):
-            block = result_v.at[i, :, inside]
-            pltpu.make_async_copy(block, block, out_send.at[i, p]).wait()
-            block = out_ref.at[part(other, 0, rows), inside]
-            pltpu.make_async_copy(block, block, out_recv.at[other, p]).wait()
-        return carry
-
     lax.fori_loop(0, CHUNKS, finish, 0)
-    lax.fori_loop(0, pieces, finish_out, 0)
+    for i in range(n_cset - 1):
+        block = active_v.at[mine, :]
+        pltpu.make_async_copy(block, block, active_send.at[i]).wait()
+        block = neighbour_v.at[mine, :]
+        pltpu.make_async_copy(block, block, sum_send.at[i]).wait()
 
 
 def local(
@@ -290,7 +323,6 @@
     half = (reach - 1) // 2
     splits, sets = split_active.shape
     width = OUTPAD // n_cset
-    pieces = width // min(width, 256)
     hbm = pl.BlockSpec(memory_space=pl.ANY)
     smem = pl.BlockSpec(memory_space=pltpu.SMEM)
     bf16 = jnp.bfloat16
@@ -302,17 +334,19 @@
         in_specs=[smem] * 3 + [hbm] * 5,
         out_specs=pl.BlockSpec(memory_space=pltpu.VMEM),
         scratch_shapes=[
-            pltpu.VMEM((rows, channels), bf16),
+            pltpu.VMEM((n_cset * rows, channels), bf16),
             pltpu.VMEM((splits, sets), jnp.int32),
             pltpu.VMEM((splits, sets), jnp.int32),
             pltpu.VMEM(table, jnp.float32),
             pltpu.VMEM(table, jnp.float32),
+            pltpu.VMEM((table[0], width), jnp.float32),
+            pltpu.VMEM((table[0], width), jnp.float32),
             pltpu.VMEM((reach, slots, TILE, TILE), bf16),
             pltpu.VMEM((reach, rows, n_cset * rows), bf16),
-            pltpu.VMEM((splits, rows, OUTPAD), bf16),
-            pltpu.VMEM((splits, channels, OUTPAD), bf16),
-            pltpu.VMEM((rows, channels), bf16),
-            pltpu.VMEM((n_cset, rows, width), bf16),
+            pltpu.VMEM((splits, n_cset * rows, width), bf16),
+            pltpu.VMEM((splits, channels, width), bf16),
+            pltpu.VMEM((splits, channels, width), bf16),
+            pltpu.VMEM((n_cset * rows, channels), bf16),
         ]
         + [pltpu.VMEM((n_cset * rows, channels), bf16)] * (2 * half + 1)
         + [
@@ -322,8 +356,11 @@
             dma((half, n_cset, CHUNKS)),
             dma((half + 1, n_cset, CHUNKS)),
             dma((half, n_cset, CHUNKS)),
-            dma((n_cset, pieces)),
-            dma((n_cset, pieces)),
+            dma((n_cset, CHUNKS)),
+            dma((n_cset,)),
+            dma((n_cset,)),
+            dma((n_cset,)),
+            dma((n_cset,)),
         ],
         compiler_params=pltpu.CompilerParams(
             collective_id=0, has_side_effects=True, vmem_limit_bytes=56 * 1024 * 1024

time: 29.2 us -> 27.5 us (0.942)
  Pallas kernels: 28.3 us -> 26.5 us
    pallas_call x1, Pallas kernels: 28.3 us -> 26.5 us  [local(): pl.pallas_call(functools.partial(kernel, n_blk, n_cset, half), out_shape=...]
where the time goes in v5:
time: 27.5 us; the launch traced here: 27.3 us
  Pallas kernels  26.5 us (96%)
  local copies, waits for them, and re-layouts  0.8 us (3%)
    pallas_call x1, Pallas kernels, local(): pl.pallas_call(functools.partial(kernel, n_blk, n_cset, half), out_shape=...  26.5 us
    unnamed x1, local copies, waits for them, and re-layouts  0.8 us

profile of v5, /device:TPU:0, one launch (start us, length us, event | category | flops | bytes accessed | tf_op | source)
XLA Modules:
  0.0 27.3 jit_solution(17969545087434814982)
XLA Ops:
  0.0 26.5 %shard_map.82 = bf16[512,512]{1,0:T(8,128)(2,1)S(1)} custom-call(s32[1,5,1,8]{3,2,1,0:T(1,128)} %bitcast.4, s32[1,5,1,8]{3,2,1,0:T(1,128)} %bitcast.5, s32[1,1,5]{2,1,0:T(1,128)} %count_s.1, bf16[256,256]{1,0:T(8,128)(2,1)} %active_h.1, bf16[256,256]{1,0:T(8,128)(2,1)} %passive_h.1, bf16[5,8,128,128]{3,2,1,0:T(8,128)(2,1)} %bitcast.3, s32[20,924]{1,0:T(8,128)} %left_h.1, ...), custom_call_target="tpu_custom_call" | custom-call | tf_op jit(solution)/shard_map/pallas_call | solution.py:331
  26.6 0.8 %copy.10 = bf16[512,512]{1,0:T(8,128)(2,1)} copy(bf16[512,512]{1,0:T(8,128)(2,1)S(1)} %shard_map.82) | data formatting | bytes 1048576

commit v6 on v5

--- a/solution.py
+++ b/solution.py
@@ -46,6 +46,7 @@
     away = (None,) + rest[half + 1 : 2 * half + 1]
     (
         local_sem,
+        tile_sem,
         own_send,
         side_send,
         sibling_send,
@@ -82,11 +83,16 @@
         pltpu.make_async_copy(left_h, left_raw, local_sem.at[0]),
         pltpu.make_async_copy(right_h, right_raw, local_sem.at[1]),
         pltpu.make_async_copy(active_h, active_v.at[mine, :], local_sem.at[2]),
-        pltpu.make_async_copy(adjacency_h, tiles_v, local_sem.at[3]),
-        pltpu.make_async_copy(passive_h, home[0].at[mine, :], local_sem.at[4]),
+        pltpu.make_async_copy(passive_h, home[0].at[mine, :], local_sem.at[3]),
     ]
-    for copy in copies:
+    for copy in copies[::-1]:
         copy.start()
+
+    def fetch(r):
+        return pltpu.make_async_copy(adjacency_h.at[r], tiles_v.at[r], tile_sem.at[r])
+
+    for r in range(2 * half + 1):
+        fetch(r).start()
     pl.semaphore_wait(barrier, len(senders))
 
     size = rows // CHUNKS
@@ -123,7 +129,7 @@
         block = ref.at[part(cset, q), :]
         pltpu.make_async_copy(block, block, sem).wait()
 
-    copies[4].wait()
+    copies[3].wait()
     def begin(q, carry):
         block = home[0].at[part(c, q), :]
         for k in range(half, 0, -1):
@@ -145,9 +151,9 @@
     left_own[...] = left_v[:, own_columns]
     right_own[...] = right_v[:, own_columns]
     copies[2].wait()
-    copies[3].wait()
 
     def assemble(r):
+        fetch(r).wait()
         for d in range(rows // TILE):
             for e in range(n_cset * rows // TILE):
                 total = jnp.zeros((TILE, TILE), jnp.bfloat16)
@@ -350,7 +356,8 @@
         ]
         + [pltpu.VMEM((n_cset * rows, channels), bf16)] * (2 * half + 1)
         + [
-            dma((5,)),
+            dma((4,)),
+            dma((reach,)),
             dma((half, CHUNKS)),
             dma((half + 1, n_cset, CHUNKS)),
             dma((half, n_cset, CHUNKS)),

time: 27.5 us -> 27.6 us (level)
  no operation moved by 1% of the time
where the time goes in v6:
time: 27.6 us; the launch traced here: 27.4 us
  Pallas kernels  26.6 us (96%)
  local copies, waits for them, and re-layouts  0.8 us (3%)
    pallas_call x1, Pallas kernels, local(): pl.pallas_call(functools.partial(kernel, n_blk, n_cset, half), out_shape=...  26.6 us
    unnamed x1, local copies, waits for them, and re-layouts  0.8 us

profile of v6, /device:TPU:0, one launch (start us, length us, event | category | flops | bytes accessed | tf_op | source)
XLA Modules:
  0.0 27.4 jit_solution(15083231447932474383)
XLA Ops:
  0.0 26.6 %shard_map.82 = bf16[512,512]{1,0:T(8,128)(2,1)S(1)} custom-call(s32[1,5,1,8]{3,2,1,0:T(1,128)} %bitcast.4, s32[1,5,1,8]{3,2,1,0:T(1,128)} %bitcast.5, s32[1,1,5]{2,1,0:T(1,128)} %count_s.1, bf16[256,256]{1,0:T(8,128)(2,1)} %active_h.1, bf16[256,256]{1,0:T(8,128)(2,1)} %passive_h.1, bf16[5,8,128,128]{3,2,1,0:T(8,128)(2,1)} %bitcast.3, s32[20,924]{1,0:T(8,128)} %left_h.1, ...), custom_call_target="tpu_custom_call" | custom-call | tf_op jit(solution)/shard_map/pallas_call | solution.py:337
  26.6 0.8 %copy.10 = bf16[512,512]{1,0:T(8,128)(2,1)} copy(bf16[512,512]{1,0:T(8,128)(2,1)S(1)} %shard_map.82) | data formatting | bytes 1048576

commit v7 on v6

--- a/solution.py
+++ b/solution.py
@@ -10,7 +10,8 @@
 OUTPAD = 1024
 TILE = 128
 CHUNKS = 4
-GROUP = 4
+GROUP = 10
+BAND = 128
 MESH = pl.DeviceIdType.MESH
 
 
@@ -36,10 +37,12 @@
     right_own,
     tiles_v,
     dense_v,
+    active_t,
+    sum_t,
+    joined_t,
     picked_v,
     choose_left_v,
     choose_right_v,
-    neighbour_v,
     *rest,
 ):
     home = rest[: half + 1]
@@ -60,11 +63,10 @@
     ) = rest[2 * half + 1 :]
     b = lax.axis_index("blk")
     c = lax.axis_index("cset")
-    channels = active_v.shape[1]
-    rows = active_v.shape[0] // n_cset
+    rows, channels = active_v.shape
     splits, sets = left_raw.shape
     width = out_ref.shape[1]
-    piece = min(width, 256)
+    bands = width // BAND
     sign = 2 * (b % 2) - 1
     sibling = (b - sign, c)
     others = [(c + i) % n_cset for i in range(1, n_cset)]
@@ -82,7 +84,7 @@
     copies = [
         pltpu.make_async_copy(left_h, left_raw, local_sem.at[0]),
         pltpu.make_async_copy(right_h, right_raw, local_sem.at[1]),
-        pltpu.make_async_copy(active_h, active_v.at[mine, :], local_sem.at[2]),
+        pltpu.make_async_copy(active_h, active_v, local_sem.at[2]),
         pltpu.make_async_copy(passive_h, home[0].at[mine, :], local_sem.at[3]),
     ]
     for copy in copies[::-1]:
@@ -148,9 +150,10 @@
     left_v[:splits, :sets] = left_raw[...].astype(jnp.float32)
     right_v[:splits, :sets] = right_raw[...].astype(jnp.float32)
     own_columns = pl.ds(pl.multiple_of(c * width, width), width)
-    left_own[...] = left_v[:, own_columns]
-    right_own[...] = right_v[:, own_columns]
+    left_own[...] = jnp.transpose(left_v[:, own_columns])
+    right_own[...] = jnp.transpose(right_v[:, own_columns])
     copies[2].wait()
+    active_t[c] = jnp.transpose(active_v[...])
 
     def assemble(r):
         fetch(r).wait()
@@ -162,35 +165,35 @@
                     total = total + jnp.where(here, tiles_v[r, t], jnp.zeros_like(total))
                 dense_v[r, d * TILE : (d + 1) * TILE, e * TILE : (e + 1) * TILE] = total
 
-    channel = lax.broadcasted_iota(jnp.int32, (channels, piece), 0).astype(jnp.bfloat16)
-    one, zero = jnp.ones(channel.shape, jnp.bfloat16), jnp.zeros(channel.shape, jnp.bfloat16)
-
-    def one_hot(table, j, columns):
-        row = jnp.broadcast_to(table[pl.ds(j, 1), columns], (16, piece)).astype(jnp.bfloat16)
-        return jnp.where(jnp.concatenate([row] * (channels // 16), axis=0) == channel, one, zero)
-
-    def pick(start):
-        for j in range(GROUP):
-            for at in range(0, width, piece):
-                inside = slice(at, at + piece)
-                left = one_hot(left_own, start + j, inside)
-                choose_left_v[start + j, :, inside] = left
-                choose_right_v[start + j, :, inside] = one_hot(right_own, start + j, inside)
-                picked = jnp.dot(active_v[mine, :], left, preferred_element_type=jnp.float32)
-                picked_v[start + j, mine, inside] = picked.astype(jnp.bfloat16)
-
-    def pick_others(start):
+    lane = lax.broadcasted_iota(jnp.int32, (BAND, 128), 1)
+    channel = [(lane + at).astype(jnp.bfloat16) for at in range(0, channels, 128)]
+    one, zero = jnp.ones((BAND, 128), jnp.bfloat16), jnp.zeros((BAND, 128), jnp.bfloat16)
+
+    def one_hot(table, band, choose):
+        for j in range(splits):
+            column = table[pl.ds(pl.multiple_of(band * BAND, BAND), BAND), j : j + 1]
+            wide = jnp.broadcast_to(column, (BAND, 128)).astype(jnp.bfloat16)
+            for n, at in enumerate(channel):
+                choose[band, j * BAND : (j + 1) * BAND, n * 128 : (n + 1) * 128] = jnp.where(
+                    wide == at, one, zero
+                )
+
+    def pick(band, cset):
+        for g in range(0, splits, GROUP):
+            inside = slice(g * BAND, (g + GROUP) * BAND)
+            picked = jnp.dot(
+                choose_left_v[band, inside, :], active_t[cset], preferred_element_type=jnp.float32
+            )
+            picked_v[cset, band, inside, :] = picked.astype(jnp.bfloat16)
+
+    def pick_own(band):
+        one_hot(left_own, band, choose_left_v)
+        one_hot(right_own, band, choose_right_v)
+        pick(band, c)
+
+    def pick_others(band):
         for other in others:
-            there = part(other, 0, rows)
-            for j in range(GROUP):
-                for at in range(0, width, piece):
-                    inside = slice(at, at + piece)
-                    picked = jnp.dot(
-                        active_v[there, :],
-                        choose_left_v[start + j, :, inside],
-                        preferred_element_type=jnp.float32,
-                    )
-                    picked_v[start + j, there, inside] = picked.astype(jnp.bfloat16)
+            pick(band, other)
 
     def side_arrived(k, q):
         for other in others:
@@ -212,11 +215,10 @@
             to_others(k, q)
             to_sibling(k, c, q)
 
-    groups = splits // GROUP
     reach = 2 * half + 1
 
     def advance(g, carry):
-        pl.when(g < groups)(functools.partial(pick, g * GROUP))
+        pl.when(g < bands)(functools.partial(pick_own, g))
 
         @pl.when((g >= 1) & (g <= CHUNKS))
         def _():
@@ -227,19 +229,19 @@
         @pl.when(g == 1)
         def _():
             for i, other in enumerate(others):
-                block = active_v.at[mine, :]
+                block = active_t.at[c]
                 send(block, block, active_send.at[i], active_recv.at[c], (b, other))
 
         pl.when(g < reach)(functools.partial(assemble, g))
         return carry
 
-    lax.fori_loop(0, max(groups, reach, CHUNKS + 1), advance, 0)
+    lax.fori_loop(0, max(bands, reach, CHUNKS + 1), advance, 0)
     for other in others:
-        block = active_v.at[part(other, 0, rows), :]
+        block = active_t.at[other]
         pltpu.make_async_copy(block, block, active_recv.at[other]).wait()
 
     def forward(g, carry):
-        pl.when(g < groups)(functools.partial(pick_others, g * GROUP))
+        pl.when(g < bands)(functools.partial(pick_others, g))
 
         @pl.when(g < CHUNKS)
         def _():
@@ -248,7 +250,7 @@
 
         return carry
 
-    lax.fori_loop(0, max(groups, CHUNKS), forward, 0)
+    lax.fori_loop(0, max(bands, CHUNKS), forward, 0)
 
     def times(r, ref):
         return jnp.dot(dense_v[r], ref[...], preferred_element_type=jnp.float32)
@@ -264,35 +266,35 @@
     for q in range(CHUNKS):
         side_arrived(half, q)
     total = total + times(half + sign * half, home[half])
-    neighbour_v[mine, :] = total.astype(jnp.bfloat16)
+    sum_t[c] = jnp.transpose(total).astype(jnp.bfloat16)
     for i, other in enumerate(others):
-        block = neighbour_v.at[mine, :]
+        block = sum_t.at[c]
         send(block, block, sum_send.at[i], sum_recv.at[c], (b, other))
-    pieces = width // piece
 
     def join(n, carry):
-        i, p = n // pieces, n % pieces
+        i, band = n // bands, n % bands
         owner = (c + i) % n_cset
-        there = part(owner, 0, rows)
-        inside = pl.ds(pl.multiple_of(p * piece, piece), piece)
-
-        @pl.when((i > 0) & (p == 0))
+
+        @pl.when((i > 0) & (band == 0))
         def _():
-            block = neighbour_v.at[there, :]
+            block = sum_t.at[owner]
             pltpu.make_async_copy(block, block, sum_recv.at[owner]).wait()
 
-        total = jnp.zeros((rows, piece), jnp.float32)
-        for j in range(splits):
+        total = jnp.zeros((BAND, rows), jnp.float32)
+        for g in range(0, splits, GROUP):
+            inside = slice(g * BAND, (g + GROUP) * BAND)
             found = jnp.dot(
-                neighbour_v[there, :],
-                choose_right_v[j, :, inside],
-                preferred_element_type=jnp.float32,
+                choose_right_v[band, inside, :], sum_t[owner], preferred_element_type=jnp.float32
             )
-            total = total + picked_v[j, there, inside].astype(jnp.float32) * found
-        out_ref[there, inside] = total.astype(jnp.bfloat16)
+            for j in range(GROUP):
+                picked = picked_v[owner, band, (g + j) * BAND : (g + j + 1) * BAND, :]
+                total = total + picked.astype(jnp.float32) * found[j * BAND : (j + 1) * BAND, :]
+        joined_t[...] = total
+        inside = pl.ds(pl.multiple_of(band * BAND, BAND), BAND)
+        out_ref[part(owner, 0, rows), inside] = jnp.transpose(joined_t[...]).astype(jnp.bfloat16)
         return carry
 
-    lax.fori_loop(0, n_cset * pieces, join, 0)
+    lax.fori_loop(0, n_cset * bands, join, 0)
 
     def finish(q, carry):
         block = home[0].at[part(c, q), :]
@@ -306,9 +308,9 @@
 
     lax.fori_loop(0, CHUNKS, finish, 0)
     for i in range(n_cset - 1):
-        block = active_v.at[mine, :]
+        block = active_t.at[c]
         pltpu.make_async_copy(block, block, active_send.at[i]).wait()
-        block = neighbour_v.at[mine, :]
+        block = sum_t.at[c]
         pltpu.make_async_copy(block, block, sum_send.at[i]).wait()
 
 
@@ -333,26 +335,28 @@
     smem = pl.BlockSpec(memory_space=pltpu.SMEM)
     bf16 = jnp.bfloat16
     dma = pltpu.SemaphoreType.DMA
-    table = (-(-splits // 8) * 8, OUTPAD)
+    table = (-(-splits // 128) * 128, OUTPAD)
     return pl.pallas_call(
         functools.partial(kernel, n_blk, n_cset, half),
         out_shape=pltpu.VMEM((n_cset * rows, width), bf16),
         in_specs=[smem] * 3 + [hbm] * 5,
         out_specs=pl.BlockSpec(memory_space=pltpu.VMEM),
         scratch_shapes=[
-            pltpu.VMEM((n_cset * rows, channels), bf16),
+            pltpu.VMEM((rows, channels), bf16),
             pltpu.VMEM((splits, sets), jnp.int32),
             pltpu.VMEM((splits, sets), jnp.int32),
             pltpu.VMEM(table, jnp.float32),
             pltpu.VMEM(table, jnp.float32),
-            pltpu.VMEM((table[0], width), jnp.float32),
-            pltpu.VMEM((table[0], width), jnp.float32),
+            pltpu.VMEM((width, table[0]), jnp.float32),
+            pltpu.VMEM((width, table[0]), jnp.float32),
             pltpu.VMEM((reach, slots, TILE, TILE), bf16),
             pltpu.VMEM((reach, rows, n_cset * rows), bf16),
-            pltpu.VMEM((splits, n_cset * rows, width), bf16),
-            pltpu.VMEM((splits, channels, width), bf16),
-            pltpu.VMEM((splits, channels, width), bf16),
-            pltpu.VMEM((n_cset * rows, channels), bf16),
+            pltpu.VMEM((n_cset, channels, rows), bf16),
+            pltpu.VMEM((n_cset, channels, rows), bf16),
+            pltpu.VMEM((BAND, rows), jnp.float32),
+            pltpu.VMEM((n_cset, width // BAND, splits * BAND, rows), bf16),
+            pltpu.VMEM((width // BAND, splits * BAND, channels), bf16),
+            pltpu.VMEM((width // BAND, splits * BAND, channels), bf16),
         ]
         + [pltpu.VMEM((n_cset * rows, channels), bf16)] * (2 * half + 1)
         + [

time: 27.6 us -> 28.8 us (1.043)
  Pallas kernels: 26.6 us -> 27.8 us
    pallas_call x1, Pallas kernels: 26.6 us -> 27.8 us  [local(): pl.pallas_call(functools.partial(kernel, n_blk, n_cset, half), out_shape=...]
where the time goes in v7:
time: 28.8 us; the launch traced here: 28.6 us
  Pallas kernels  27.8 us (97%)
  local copies, waits for them, and re-layouts  0.8 us (3%)
    pallas_call x1, Pallas kernels, local(): pl.pallas_call(functools.partial(kernel, n_blk, n_cset, half), out_shape=...  27.8 us
    unnamed x1, local copies, waits for them, and re-layouts  0.8 us

profile of v7, /device:TPU:0, one launch (start us, length us, event | category | flops | bytes accessed | tf_op | source)
XLA Modules:
  0.0 28.6 jit_solution(5259075402478448968)
XLA Ops:
  0.0 27.8 %shard_map.82 = bf16[512,512]{1,0:T(8,128)(2,1)S(1)} custom-call(s32[1,5,1,8]{3,2,1,0:T(1,128)} %bitcast.4, s32[1,5,1,8]{3,2,1,0:T(1,128)} %bitcast.5, s32[1,1,5]{2,1,0:T(1,128)} %count_s.1, bf16[256,256]{1,0:T(8,128)(2,1)} %active_h.1, bf16[256,256]{1,0:T(8,128)(2,1)} %passive_h.1, bf16[5,8,128,128]{3,2,1,0:T(8,128)(2,1)} %bitcast.3, s32[20,924]{1,0:T(8,128)} %left_h.1, ...), custom_call_target="tpu_custom_call" | custom-call | tf_op jit(solution)/shard_map/pallas_call | solution.py:339
  27.8 0.8 %copy.10 = bf16[512,512]{1,0:T(8,128)(2,1)} copy(bf16[512,512]{1,0:T(8,128)(2,1)S(1)} %shard_map.82) | data formatting | bytes 1048576

commit v8 on v6

--- a/solution.py
+++ b/solution.py
@@ -9,7 +9,7 @@
 
 OUTPAD = 1024
 TILE = 128
-CHUNKS = 4
+CHUNKS = 2
 GROUP = 4
 MESH = pl.DeviceIdType.MESH
 

time: 27.6 us -> 27.2 us (0.986)
  Pallas kernels: 26.6 us -> 26.2 us
    pallas_call x1, Pallas kernels: 26.6 us -> 26.2 us  [local(): pl.pallas_call(functools.partial(kernel, n_blk, n_cset, half), out_shape=...]
where the time goes in v8:
time: 27.2 us; the launch traced here: 27 us
  Pallas kernels  26.2 us (96%)
  local copies, waits for them, and re-layouts  0.8 us (3%)
    pallas_call x1, Pallas kernels, local(): pl.pallas_call(functools.partial(kernel, n_blk, n_cset, half), out_shape=...  26.2 us
    unnamed x1, local copies, waits for them, and re-layouts  0.8 us

profile of v8, /device:TPU:0, one launch (start us, length us, event | category | flops | bytes accessed | tf_op | source)
XLA Modules:
  0.0 27.0 jit_solution(2507796391462308445)
XLA Ops:
  0.0 26.2 %shard_map.82 = bf16[512,512]{1,0:T(8,128)(2,1)S(1)} custom-call(s32[1,5,1,8]{3,2,1,0:T(1,128)} %bitcast.4, s32[1,5,1,8]{3,2,1,0:T(1,128)} %bitcast.5, s32[1,1,5]{2,1,0:T(1,128)} %count_s.1, bf16[256,256]{1,0:T(8,128)(2,1)} %active_h.1, bf16[256,256]{1,0:T(8,128)(2,1)} %passive_h.1, bf16[5,8,128,128]{3,2,1,0:T(8,128)(2,1)} %bitcast.3, s32[20,924]{1,0:T(8,128)} %left_h.1, ...), custom_call_target="tpu_custom_call" | custom-call | tf_op jit(solution)/shard_map/pallas_call | solution.py:337
  26.2 0.8 %copy.10 = bf16[512,512]{1,0:T(8,128)(2,1)} copy(bf16[512,512]{1,0:T(8,128)(2,1)S(1)} %shard_map.82) | data formatting | bytes 1048576
